TPU v7x, 32 devices: a whole 2x2x4 slice. The times are simulated.
32 devices in a mesh: grp: 2 (over y), ep: 16 (over z, x, core), tp: 1.
Axes of the slice: x: 2, y: 2, z: 4, core: 2. Of those that a mesh axis runs over, the one named last changes fastest.
Arguments:
- hidden_in: bfloat16 [2, 256, 2048], P(None, ('grp', 'ep')), parts along dimension 1, may hold values from -6 to 6
- routes: int32 [2, 256, 8], P(None, ('grp', 'ep')), parts along dimension 1, may hold values from 0 to 7, all different within a row; in each aligned block of 8 rows (0 to 7, 8 to 15, ..., all dimensions but the last counted through in order) at most 8 rows name the same one
- gates: float32 [2, 256, 8], P(None, ('grp', 'ep')), parts along dimension 1, may hold values from 0.1 to 1
- query: bfloat16 [2, 256, 8192], P(None, ('grp', 'ep'), 'tp'), parts along dimension 1, may hold values from -13 to 13
- cached_key_rows: bfloat16 [2, 256, 64, 512], P(None, ('grp', 'ep'), None, 'tp'), parts along dimension 1, may hold values from -4 to 4
- cached_value_rows: bfloat16 [2, 256, 64, 512], P(None, ('grp', 'ep'), None, 'tp'), parts along dimension 1, may hold values from -4 to 4
- fresh_key: bfloat16 [2, 256, 512], P(None, ('grp', 'ep'), 'tp'), parts along dimension 1, may hold values from -4 to 4
- fresh_value: bfloat16 [2, 256, 512], P(None, ('grp', 'ep'), 'tp'), parts along dimension 1, may hold values from -4 to 4
- lengths: int32 [2, 256], P(None, ('grp', 'ep')), parts along dimension 1, may hold values from 2 to 64, as said below
- w_gate: bfloat16 [16, 2048, 384], P('ep', None, 'tp'), may hold values from -0.125 to 0.125
- w_up: bfloat16 [16, 2048, 384], P('ep', None, 'tp'), may hold values from -0.125 to 0.125
- w_down: bfloat16 [16, 384, 2048], P('ep', 'tp'), may hold values from -0.21875 to 0.21875
Outputs:
- attn_out: bfloat16 [2, 256, 8192], P(None, ('grp', 'ep'), 'tp'), parts along dimension 1
- moe_out: bfloat16 [2, 256, 2048], P(None, ('grp', 'ep'), 'tp'), parts along dimension 1
There are 2 independent parts, one for each index of `grp`. A program takes and returns all parts, laid end to end along the dimension named above; an argument that names none is the same for every part. Nothing has to cross between parts.
Inputs may be any that keep to these rules, and one draw needn't show every extreme that they name: `routes`: in each micro-batch no expert is named by more than 8 of the 8 rows of one index of ep, a bound that some block reaches of them; a row names 8 different experts. `lengths`: some row has all 64 positions live.
All inputs are finite; a program needn't handle non-finite values.
Results may differ from a plain program's by a relative error of at most 0.0057.
Values may be sent and summed in bfloat16 or wider, within the bound.
A program may use at most 64 MiB of HBM per device.

v0:
```python
import math

import jax
import jax.numpy as jnp
from jax import lax
from jax.sharding import PartitionSpec as P

QUERY_HEADS = 64
KEY_VALUE_HEADS = 4
HEAD_SIZE = 128


def swapped(block, axis, bit):
    count = lax.axis_size(axis)
    route = []
    for low in range(count):
        high = low | 1 << bit
        if high != low and high < count:
            route += [(low, high), (high, low)]
    return lax.ppermute(block, axis, route)


def attend_local(query_rows, cached_key_rows, cached_value_rows, fresh_key, fresh_value, lengths):
    row_count = query_rows.shape[0]
    query_group = QUERY_HEADS // KEY_VALUE_HEADS
    kv_local = cached_key_rows.shape[2] // HEAD_SIZE
    cache_len = cached_key_rows.shape[1]
    grouped_query_rows = query_rows.reshape(row_count, kv_local, query_group, HEAD_SIZE)
    earlier_keys = cached_key_rows.reshape(row_count, cache_len, kv_local, HEAD_SIZE)
    earlier_values = cached_value_rows.reshape(row_count, cache_len, kv_local, HEAD_SIZE)
    token_own_keys = fresh_key.reshape(row_count, kv_local, HEAD_SIZE)
    token_own_values = fresh_value.reshape(row_count, kv_local, HEAD_SIZE).astype(jnp.float32)
    score_scale = 1.0 / math.sqrt(HEAD_SIZE)
    past_score = (
        jnp.einsum(
            "rkgd,rckd->rkgc", grouped_query_rows, earlier_keys, preferred_element_type=jnp.float32
        )
        * score_scale
    )
    own_score = (
        jnp.einsum(
            "rkgd,rkd->rkg", grouped_query_rows, token_own_keys, preferred_element_type=jnp.float32
        )[..., None]
        * score_scale
    )
    valid_pos = lax.broadcasted_iota(jnp.int32, (row_count, cache_len), 1) < lengths[:, None]
    past_score = jnp.where(valid_pos[:, None, None, :], past_score, -jnp.inf)
    scores = jnp.concatenate([past_score, own_score], axis=-1)
    row_max = jnp.max(scores, axis=-1, keepdims=True)
    exp_scores = jnp.exp(scores - row_max)
    weights_bf = (exp_scores / jnp.sum(exp_scores, axis=-1, keepdims=True)).astype(jnp.bfloat16)
    attended = jnp.einsum(
        "rkgc,rckd->rkgd",
        weights_bf[..., :cache_len],
        earlier_values,
        preferred_element_type=jnp.float32,
    )
    attended = (
        attended + weights_bf[..., cache_len:].astype(jnp.float32) * token_own_values[:, :, None, :]
    )
    return attended.reshape(row_count, kv_local * query_group * HEAD_SIZE).astype(jnp.bfloat16)


def slot_layout(route_rows, experts, capacity):
    flat_routes = route_rows.reshape(-1)
    onehot = (flat_routes[:, None] == jnp.arange(experts, dtype=jnp.int32)[None, :]).astype(
        jnp.int32
    )
    before = jnp.cumsum(onehot, axis=0) - onehot
    slot_rank = jnp.sum(before * onehot, axis=1)
    return 2 * flat_routes * capacity + slot_rank


def pack_rows(tokens, first_slot, capacity, slot_total, route_count):
    targets = jnp.stack([first_slot, first_slot + capacity], axis=1)
    slot_ids = lax.broadcasted_iota(jnp.int32, (slot_total, 1, 1), 0)
    chosen = jnp.sum((targets[None, :, :] == slot_ids).astype(jnp.float32), axis=2)
    chosen = jnp.sum(chosen.reshape(slot_total, -1, route_count), axis=2).astype(jnp.bfloat16)
    return jnp.dot(chosen, tokens, preferred_element_type=jnp.float32).astype(jnp.bfloat16)


def combine_rows(returned, first_slot, capacity, row_gates, row_count, route_count):
    flat_back = returned.reshape(returned.shape[0] * returned.shape[1], returned.shape[2])
    lower = jnp.take(flat_back, first_slot, axis=0)
    upper = jnp.take(flat_back, first_slot + capacity, axis=0)
    outputs = jnp.concatenate([lower, upper], axis=1)
    outputs = lax.optimization_barrier(outputs).astype(jnp.float32)
    weighted = row_gates.reshape(-1, 1) * outputs
    return jnp.sum(weighted.reshape(row_count, route_count, -1), axis=1).astype(jnp.bfloat16)


def shards(
    hidden_in,
    routes,
    gates,
    query,
    cached_key_rows,
    cached_value_rows,
    fresh_key,
    fresh_value,
    lengths,
    w_gate,
    w_up,
    w_down,
):
    ep_size = lax.axis_size("ep")
    experts = ep_size // 2
    batches, row_count, route_count = routes.shape
    model_width = hidden_in.shape[2]
    capacity = min(row_count, 2 * ((row_count * route_count + experts - 1) // experts))
    slot_total = ep_size * capacity
    layouts = []
    buffers = []
    for batch_idx in range(batches):
        first_slot = slot_layout(routes[batch_idx], experts, capacity)
        layouts.append(first_slot)
        packed = pack_rows(hidden_in[batch_idx], first_slot, capacity, slot_total, route_count)
        buffers.append(packed.reshape(ep_size, capacity, model_width))
    attn_list = []
    blocks = []
    for batch_idx in range(batches):
        received = lax.all_to_all(buffers[batch_idx], "ep", split_axis=0, concat_axis=0, tiled=True)
        item_count = received.shape[1]
        slot_rows = received.reshape(ep_size * item_count, model_width)
        gate_val = jnp.dot(slot_rows, w_gate[0], preferred_element_type=jnp.float32)
        up_val = jnp.dot(slot_rows, w_up[0], preferred_element_type=jnp.float32)
        hidden = (jax.nn.silu(gate_val) * up_val).astype(jnp.bfloat16)
        partial_value = jnp.dot(hidden, w_down[0], preferred_element_type=jnp.float32)
        partial_value = partial_value.reshape(ep_size, item_count, model_width)
        half_sum = lax.psum_scatter(partial_value, "tp", scatter_dimension=2, tiled=True)
        partner = swapped(half_sum, "ep", 0)
        finished = (half_sum + partner).astype(jnp.bfloat16)
        quarter = finished.shape[2] // 2
        parity = lax.axis_index("ep") % 2
        quarter_cols = lax.dynamic_slice_in_dim(finished, parity * quarter, quarter, 2)
        blocks.append(lax.all_to_all(quarter_cols, "ep", split_axis=0, concat_axis=0, tiled=True))
        attn_list.append(
            attend_local(
                query[batch_idx],
                cached_key_rows[batch_idx],
                cached_value_rows[batch_idx],
                fresh_key[batch_idx],
                fresh_value[batch_idx],
                lengths[batch_idx],
            )
        )
    moe_list = []
    for batch_idx in range(batches):
        moe_list.append(
            combine_rows(
                blocks[batch_idx],
                layouts[batch_idx],
                capacity,
                gates[batch_idx],
                row_count,
                route_count,
            )
        )
    return (jnp.stack(attn_list), jnp.stack(moe_list))


def solution(mesh):
    in_specs = (
        P(None, ("grp", "ep"), None),
        P(None, ("grp", "ep"), None),
        P(None, ("grp", "ep"), None),
        P(None, ("grp", "ep"), "tp"),
        P(None, ("grp", "ep"), None, "tp"),
        P(None, ("grp", "ep"), None, "tp"),
        P(None, ("grp", "ep"), "tp"),
        P(None, ("grp", "ep"), "tp"),
        P(None, ("grp", "ep")),
        P("ep", None, "tp"),
        P("ep", None, "tp"),
        P("ep", "tp", None),
    )
    out_specs = (P(None, ("grp", "ep"), "tp"), P(None, ("grp", "ep"), "tp"))
    return jax.shard_map(shards, mesh=mesh, in_specs=in_specs, out_specs=out_specs, check_vma=False)
```

profile of v0, /device:TPU:0, one launch (start us, length us, event | category | flops | bytes accessed | tf_op | source)
XLA Modules:
  0.0 86.2 jit_solution(6629981767250306115)
XLA Ops:
  0.7 1.4 %fusion.91 = (s32[1,8,8]{2,1,0:T(8,128)S(1)}, s32[1,8,8]{2,1,0:T(8,128)S(1)}, s32[1,8,8]{2,1,0:T(8,128)}, s32[1,8,8]{2,1,0:T(8,128)}) fusion(s32[2,8,8]{2,1,0:T(8,128)} %param.15), kind=kLoop, calls=%fused_computation.151 | loop fusion | flops 128 | bytes 1536 | tf_op jit(solution)/shard_map/slice | solution.py:115
  2.8 1.9 %fusion = bf16[16,8,2048]{2,1,0:T(8,128)(2,1)} fusion(bf16[2,8,2048]{2,1,0:T(8,128)(2,1)} %param.14, bf16[128,8]{0,1:T(8,128)(2,1)S(1)} %bitcast_reduce_fusion.3), kind=kOutput, calls=%fused_computation.6 | convolution fusion | flops 4456448 | bytes 559104 | tf_op jit(solution)/shard_map/dot_general | solution.py:79
  4.6 7.4 %all-to-all-start = ((bf16[16,8,2048]{2,1,0:T(8,128)(2,1)}), bf16[16,8,2048]{2,1,0:T(8,128)(2,1)}, u32[]{:S(2)}, u32[]{:S(2)}) async-start(bf16[16,8,2048]{2,1,0:T(8,128)(2,1)} %fusion), calls=%async_computation | async-start | bytes 1048576 | tf_op jit(solution)/shard_map/all_to_all | solution.py:122
  12.2 2.1 %fusion.88 = (bf16[1,8,64,512]{3,2,1,0:T(8,128)(2,1)S(1)}, bf16[1,8,64,512]{3,2,1,0:T(8,128)(2,1)}) fusion(bf16[2,8,64,512]{3,2,1,0:T(8,128)(2,1)} %param.18), kind=kLoop, calls=%fused_computation.148 | loop fusion | bytes 2097152 | tf_op jit(solution)/shard_map/slice | solution.py:140
  14.8 0.4 copy.116
  15.2 1.2 %reshape_squeeze.35 = bf16[8,64,4,128]{3,2,1,0:T(4,128)(2,1)S(1)} reshape(bf16[1,8,64,512]{3,2,1,0:T(8,128)(2,1)} %get-tuple-element.20) | data formatting | bytes 1048576 | tf_op jit(solution)/shard_map/reshape;squeeze | solution.py:29
  16.4 0.4 fusion.52
  16.8 1.3 %copy.125 = f32[8,4,16,64]{2,0,3,1:T(8,128)} copy(f32[8,4,16,64]{3,2,1,0:T(8,128)S(1)} %fusion.52) | data formatting | bytes 262144 | tf_op jit(solution)/shard_map/rkgd,rckd->rkgc/dot_general | solution.py:35
  18.4 1.6 %fusion.86 = (f32[8,4,16]{2,0,1:T(8,128)S(1)}, f32[8,4,16,64]{2,0,3,1:T(8,128)S(1)}, f32[8,4,16]{2,0,1:T(8,128)S(1)}, f32[8,4,16,64]{2,0,3,1:T(8,128)S(1)}) fusion(f32[8,4,16,64]{2,0,3,1:T(8,128)S(1)} %copy.116, pred[8,64]{0,1:T(8,128)(4,1)S(1)} %iota_compare_fusion.5, f32[8,4,16,64]{2,0,3,1:T(8,128)} %copy.125, pred[8,64]{0,1:T(8,128)(4,1)S(1)} %iota_compare_fusion.4), kind=kLoop, calls=%fused_computation.146 | loop fusion | flops 195584 | bytes 529408 | tf_op jit(solution)/shard_map/reduce_max | solution.py:49
  21.6 0.4 copy-done.11
  22.3 2.1 %fusion.89 = (bf16[1,8,64,512]{3,2,1,0:T(8,128)(2,1)}, bf16[1,8,64,512]{3,2,1,0:T(8,128)(2,1)S(1)}) fusion(bf16[2,8,64,512]{3,2,1,0:T(8,128)(2,1)} %param.19), kind=kLoop, calls=%fused_computation.149 | loop fusion | bytes 2097152 | tf_op jit(solution)/shard_map/slice | solution.py:141
  24.5 1.2 %reshape_squeeze.33 = bf16[8,64,4,128]{3,2,1,0:T(4,128)(2,1)S(1)} reshape(bf16[1,8,64,512]{3,2,1,0:T(8,128)(2,1)} %get-tuple-element.21) | data formatting | bytes 1048576 | tf_op jit(solution)/shard_map/reshape;squeeze | solution.py:30
  26.3 0.8 slice-done.1
  27.8 1.2 %fusion.1 = bf16[16,8,2048]{2,1,0:T(8,128)(2,1)} fusion(bf16[2,8,2048]{2,1,0:T(8,128)(2,1)S(1)} %copy-done.7, bf16[128,8]{0,1:T(8,128)(2,1)S(1)} %bitcast_reduce_fusion.2), kind=kOutput, calls=%fused_computation.7 | convolution fusion | flops 4456448 | bytes 559104 | tf_op jit(solution)/shard_map/dot_general | solution.py:79
  29.0 6.0 %all-to-all-start.2 = ((bf16[16,8,2048]{2,1,0:T(8,128)(2,1)}), bf16[16,8,2048]{2,1,0:T(8,128)(2,1)}, u32[]{:S(2)}, u32[]{:S(2)}) async-start(bf16[16,8,2048]{2,1,0:T(8,128)(2,1)} %fusion.1), calls=%async_computation.2 | async-start | bytes 1048576 | tf_op jit(solution)/shard_map/all_to_all | solution.py:122
  35.0 0.7 pad_maximum_fusion
  35.7 1.5 %fusion.12 = f32[128,384]{1,0:T(8,128)S(1)} fusion(bf16[1,2048,384]{2,1,0:T(8,128)(2,1)S(1)} %copy-done.1, bf16[16,8,2048]{2,1,0:T(8,128)(2,1)} %all-to-all-done), kind=kOutput, calls=%fused_computation.18 | convolution fusion | flops 201326592 | bytes 2293760 | tf_op jit(solution)/shard_map/dot_general | solution.py:125
  37.2 3.4 %fusion.4 = f32[16,8,2048]{2,1,0:T(8,128)} fusion(bf16[1,384,2048]{2,1,0:T(8,128)(2,1)S(1)} %copy-done, bf16[1,2048,384]{2,1,0:T(8,128)(2,1)} %param.24, bf16[16,8,2048]{2,1,0:T(8,128)(2,1)} %all-to-all-done, f32[128,384]{1,0:T(8,128)S(1)} %fusion.12), kind=kOutput, calls=%fused_computation.10 | convolution fusion | flops 402948096 | bytes 4915200 | tf_op jit(solution)/shard_map/dot_general | solution.py:128
  40.9 8.6 %all-to-all-done.2 = bf16[16,8,2048]{2,1,0:T(8,128)(2,1)} async-done(((bf16[16,8,2048]{2,1,0:T(8,128)(2,1)}), bf16[16,8,2048]{2,1,0:T(8,128)(2,1)}, u32[]{:S(2)}, u32[]{:S(2)}) %all-to-all-start.2) | async-done | bytes 524320 | tf_op jit(solution)/shard_map/all_to_all | solution.py:122
  49.5 1.5 %fusion.10 = f32[128,384]{1,0:T(8,128)S(1)} fusion(bf16[1,2048,384]{2,1,0:T(8,128)(2,1)S(1)} %copy-done.1, bf16[16,8,2048]{2,1,0:T(8,128)(2,1)} %all-to-all-done.2), kind=kOutput, calls=%fused_computation.16 | convolution fusion | flops 201326592 | bytes 2293760 | tf_op jit(solution)/shard_map/dot_general | solution.py:125
  51.0 2.4 %fusion.2 = f32[16,8,2048]{2,1,0:T(8,128)S(1)} fusion(bf16[1,384,2048]{2,1,0:T(8,128)(2,1)S(1)} %copy-done, bf16[1,2048,384]{2,1,0:T(8,128)(2,1)} %param.24, bf16[16,8,2048]{2,1,0:T(8,128)(2,1)} %all-to-all-done.2, f32[128,384]{1,0:T(8,128)S(1)} %fusion.10), kind=kOutput, calls=%fused_computation.8 | convolution fusion | flops 402948096 | bytes 4915200 | tf_op jit(solution)/shard_map/dot_general | solution.py:128
  53.6 2.0 %fusion.43 = bf16[16,8,1024]{2,1,0:T(8,128)(2,1)} fusion(f32[16,8,2048]{2,1,0:T(8,128)} %collective-permute-done, s32[]{:T(128)S(6)} %select_n.30, f32[16,8,2048]{2,1,0:T(8,128)} %fusion.4), kind=kLoop, calls=%fused_computation.43 | loop fusion | flops 262144 | bytes 1310724 | tf_op jit(solution)/shard_map/convert_element_type | solution.py:132
  55.6 4.4 %all-to-all-start.1 = ((bf16[16,8,1024]{2,1,0:T(8,128)(2,1)}), bf16[16,8,1024]{2,1,0:T(8,128)(2,1)S(1)}, u32[]{:S(2)}, u32[]{:S(2)}) async-start(bf16[16,8,1024]{2,1,0:T(8,128)(2,1)} %fusion.43), calls=%async_computation.1 | async-start | bytes 524288 | tf_op jit(solution)/shard_map/all_to_all | solution.py:136
  60.0 1.8 %fusion.42 = bf16[16,8,1024]{2,1,0:T(8,128)(2,1)} fusion(f32[16,8,2048]{2,1,0:T(8,128)} %collective-permute-done.1, s32[]{:T(128)S(6)} %select_n.30, f32[16,8,2048]{2,1,0:T(8,128)S(1)} %fusion.2), kind=kLoop, calls=%fused_computation.41 | loop fusion | flops 262144 | bytes 1310724 | tf_op jit(solution)/shard_map/convert_element_type | solution.py:132
  61.8 8.2 %all-to-all-done.1 = bf16[16,8,1024]{2,1,0:T(8,128)(2,1)S(1)} async-done(((bf16[16,8,1024]{2,1,0:T(8,128)(2,1)}), bf16[16,8,1024]{2,1,0:T(8,128)(2,1)S(1)}, u32[]{:S(2)}, u32[]{:S(2)}) %all-to-all-start.1) | async-done | bytes 262176 | tf_op jit(solution)/shard_map/all_to_all | solution.py:136
  70.0 3.5 %all-to-all-start.3 = ((bf16[16,8,1024]{2,1,0:T(8,128)(2,1)}), bf16[16,8,1024]{2,1,0:T(8,128)(2,1)S(1)}, u32[]{:S(2)}, u32[]{:S(2)}) async-start(bf16[16,8,1024]{2,1,0:T(8,128)(2,1)} %fusion.42), calls=%async_computation.3 | async-start | bytes 524288 | tf_op jit(solution)/shard_map/all_to_all | solution.py:136
  73.7 0.7 gather_fusion
  74.4 0.7 gather_fusion.1
  75.2 8.3 %all-to-all-done.3 = bf16[16,8,1024]{2,1,0:T(8,128)(2,1)S(1)} async-done(((bf16[16,8,1024]{2,1,0:T(8,128)(2,1)}), bf16[16,8,1024]{2,1,0:T(8,128)(2,1)S(1)}, u32[]{:S(2)}, u32[]{:S(2)}) %all-to-all-start.3) | async-done | bytes 262176 | tf_op jit(solution)/shard_map/all_to_all | solution.py:136
  83.5 0.7 gather_fusion.2
  84.2 0.7 gather_fusion.3
  85.6 0.6 pad_maximum_fusion.3
  (109 shorter events, 5.8 us)
Async XLA Ops:
  0.6 36.6 %copy-start = (bf16[1,384,2048]{2,1,0:T(8,128)(2,1)S(1)}, bf16[1,384,2048]{2,1,0:T(8,128)(2,1)}, u32[]{:S(2)}) copy-start(bf16[1,384,2048]{2,1,0:T(8,128)(2,1)} %param.25) | copy-start | bytes 4718596
  0.6 11.4 %copy-start.6 = (bf16[2,8,8192]{2,1,0:T(8,128)(2,1)S(1)}, bf16[2,8,8192]{2,1,0:T(8,128)(2,1)}, u32[]{:S(2)}) copy-start(bf16[2,8,8192]{2,1,0:T(8,128)(2,1)} %param.17) | copy-start | bytes 786436
  2.2 9.9 %copy-start.12 = (s32[64]{0:T(128)}, s32[64]{0:T(128)S(1)}, u32[]{:S(2)}) copy-start(s32[64]{0:T(128)S(1)} %eq.59) | copy-start | bytes 772
  2.5 9.6 %copy-start.15 = (s32[64]{0:T(128)}, s32[64]{0:T(128)S(1)}, u32[]{:S(2)}) copy-start(s32[64]{0:T(128)S(1)} %select_reduce_fusion.1) | copy-start | bytes 772
  4.6 24.4 %all-to-all-start = ((bf16[16,8,2048]{2,1,0:T(8,128)(2,1)}), bf16[16,8,2048]{2,1,0:T(8,128)(2,1)}, u32[]{:S(2)}, u32[]{:S(2)}) async-start(bf16[16,8,2048]{2,1,0:T(8,128)(2,1)} %fusion), calls=%async_computation | async-start | bytes 1048576 | tf_op jit(solution)/shard_map/all_to_all | solution.py:122
  12.1 2.3 %copy-start.4 = (bf16[1,8,64,128]{3,2,1,0:T(8,128)(2,1)}, bf16[1,8,64,128]{3,2,1,0:T(8,128)(2,1)S(1)}, u32[]{:S(2)}) copy-start(bf16[1,8,64,128]{3,2,1,0:T(8,128)(2,1)S(1)} %copy.139) | copy-start | bytes 393220
  16.4 1.8 %copy-start.9 = (bf16[2,8,512]{2,1,0:T(8,128)(2,1)S(1)}, bf16[2,8,512]{2,1,0:T(8,128)(2,1)}, u32[]{:S(2)}) copy-start(bf16[2,8,512]{2,1,0:T(8,128)(2,1)} %param.20) | copy-start | bytes 49156
  16.8 1.4 %copy-start.17 = (s32[2,8]{1,0:T(2,128)S(1)}, s32[2,8]{1,0:T(2,128)}, u32[]{:S(2)}) copy-start(s32[2,8]{1,0:T(2,128)} %param.22) | copy-start | bytes 196
  16.8 1.4 %copy-start.5 = (bf16[1,8,64,128]{3,2,1,0:T(8,128)(2,1)S(1)}, bf16[1,8,64,128]{3,2,1,0:T(8,128)(2,1)}, u32[]{:S(2)}) copy-start(bf16[1,8,64,128]{3,2,1,0:T(8,128)(2,1)} %copy-done.4) | copy-start | bytes 393220
  20.5 0.8 copy-start.2
  21.3 0.7 copy-start.11
  21.3 0.9 %copy-start.10 = (s32[1,8,8]{2,1,0:T(8,128)S(1)}, s32[1,8,8]{2,1,0:T(8,128)}, u32[]{:S(2)}) copy-start(s32[1,8,8]{2,1,0:T(8,128)} %get-tuple-element.37) | copy-start | bytes 772
  21.5 2.9 %copy-start.3 = (bf16[8,4,16,65]{2,0,3,1:T(8,128)(2,1)}, bf16[8,4,16,65]{2,0,3,1:T(8,128)(2,1)S(1)}, u32[]{:S(2)}) copy-start(bf16[8,4,16,65]{2,0,3,1:T(8,128)(2,1)S(1)} %divide_convert_fusion) | copy-start | bytes 199684
  22.3 3.4 %copy-start.8 = (bf16[2,8,512]{2,1,0:T(8,128)(2,1)S(1)}, bf16[2,8,512]{2,1,0:T(8,128)(2,1)}, u32[]{:S(2)}) copy-start(bf16[2,8,512]{2,1,0:T(8,128)(2,1)} %param.21) | copy-start | bytes 49156
  24.5 1.3 %slice-start = ((bf16[8,4,16,65]{2,0,3,1:T(8,128)(2,1)}), bf16[8,4,16,64]{2,0,3,1:T(8,128)(2,1)S(1)}, s32[]{:S(2)}) async-start(bf16[8,4,16,65]{2,0,3,1:T(8,128)(2,1)} %copy-done.2), calls=%async_computation.4 | async-start | bytes 1048576 | tf_op jit(solution)/shard_map/slice | solution.py:54
  26.1 1.0 %slice-start.1 = ((bf16[8,4,16,65]{2,0,3,1:T(8,128)(2,1)}), bf16[8,4,16,64]{2,0,3,1:T(8,128)(2,1)S(1)}, s32[]{:S(2)}) async-start(bf16[8,4,16,65]{2,0,3,1:T(8,128)(2,1)} %copy-done.3), calls=%async_computation.5 | async-start | bytes 1048576 | tf_op jit(solution)/shard_map/slice | solution.py:54
  26.3 1.5 %copy-start.7 = (bf16[2,8,2048]{2,1,0:T(8,128)(2,1)S(1)}, bf16[2,8,2048]{2,1,0:T(8,128)(2,1)}, u32[]{:S(2)}) copy-start(bf16[2,8,2048]{2,1,0:T(8,128)(2,1)} %param.14) | copy-start | bytes 196612
  27.8 7.9 %copy-start.1 = (bf16[1,2048,384]{2,1,0:T(8,128)(2,1)S(1)}, bf16[1,2048,384]{2,1,0:T(8,128)(2,1)}, u32[]{:S(2)}) copy-start(bf16[1,2048,384]{2,1,0:T(8,128)(2,1)} %param.23) | copy-start | bytes 4718596
  29.0 20.5 %all-to-all-start.2 = ((bf16[16,8,2048]{2,1,0:T(8,128)(2,1)}), bf16[16,8,2048]{2,1,0:T(8,128)(2,1)}, u32[]{:S(2)}, u32[]{:S(2)}) async-start(bf16[16,8,2048]{2,1,0:T(8,128)(2,1)} %fusion.1), calls=%async_computation.2 | async-start | bytes 1048576 | tf_op jit(solution)/shard_map/all_to_all | solution.py:122
  40.6 13.0 %collective-permute-start = (f32[16,8,2048]{2,1,0:T(8,128)}, f32[16,8,2048]{2,1,0:T(8,128)}, u32[]{:S(2)}, u32[]{:S(2)}) collective-permute-start(f32[16,8,2048]{2,1,0:T(8,128)} %fusion.4), channel_id=1, source_target_pairs={{0,1},{1,0},{2,3},{3,2},{4,5},{5,4},{6,7},{7,6},{8,9},{9,8},{10,11... | collective-permute-start | bytes 3145736 | tf_op jit(solution)/shard_map/ppermute | solution.py:20
  51.0 2.5 %copy-start.13 = (s32[64]{0:T(128)S(1)}, s32[64]{0:T(128)}, u32[]{:S(2)}) copy-start(s32[64]{0:T(128)} %copy-done.12) | copy-start | bytes 772
  51.0 2.5 %copy-start.16 = (s32[64]{0:T(128)S(1)}, s32[64]{0:T(128)}, u32[]{:S(2)}) copy-start(s32[64]{0:T(128)} %copy-done.15) | copy-start | bytes 772
  53.4 6.5 %copy-start.14 = (f32[2,8,8]{2,1,0:T(8,128)S(1)}, f32[2,8,8]{2,1,0:T(8,128)}, u32[]{:S(2)}) copy-start(f32[2,8,8]{2,1,0:T(8,128)} %param.16) | copy-start | bytes 1540
  53.4 6.6 %collective-permute-start.1 = (f32[16,8,2048]{2,1,0:T(8,128)S(1)}, f32[16,8,2048]{2,1,0:T(8,128)}, u32[]{:S(2)}, u32[]{:S(2)}) collective-permute-start(f32[16,8,2048]{2,1,0:T(8,128)S(1)} %fusion.2), channel_id=1, source_target_pairs={{0,1},{1,0},{2,3},{3,2},{4,5},{5,4},{6,7},{7,6},{8,9},{9,8},{10,11... | collective-permute-start | bytes 3145736 | tf_op jit(solution)/shard_map/ppermute | solution.py:20
  55.6 14.4 %all-to-all-start.1 = ((bf16[16,8,1024]{2,1,0:T(8,128)(2,1)}), bf16[16,8,1024]{2,1,0:T(8,128)(2,1)S(1)}, u32[]{:S(2)}, u32[]{:S(2)}) async-start(bf16[16,8,1024]{2,1,0:T(8,128)(2,1)} %fusion.43), calls=%async_computation.1 | async-start | bytes 524288 | tf_op jit(solution)/shard_map/all_to_all | solution.py:136
  70.0 13.5 %all-to-all-start.3 = ((bf16[16,8,1024]{2,1,0:T(8,128)(2,1)}), bf16[16,8,1024]{2,1,0:T(8,128)(2,1)S(1)}, u32[]{:S(2)}, u32[]{:S(2)}) async-start(bf16[16,8,1024]{2,1,0:T(8,128)(2,1)} %fusion.42), calls=%async_computation.3 | async-start | bytes 524288 | tf_op jit(solution)/shard_map/all_to_all | solution.py:136
where the time goes:
time: 87.3 us; the launch traced here: 86.2 us
  waiting for transfers between devices  25.1 us (29%)
  starting transfers between devices  21.8 us (25%)
  local copies, waits for them, and re-layouts  13.8 us (16%)
  matrix products  13.5 us (15%)
  other arithmetic  10.9 us (12%)
  between operations  1.27 us (1%)
    all_to_all x2, waiting for transfers between devices, shards(): lax.all_to_all(quarter_cols, 'ep', split_axis=0, concat_axis=0, tiled=True)  16.5 us
    all_to_all x2, starting transfers between devices, shards(): lax.all_to_all(buffers[batch_idx], 'ep', split_axis=0, concat_axis=0, til...  13.4 us
    all_to_all x2, waiting for transfers between devices, shards(): lax.all_to_all(buffers[batch_idx], 'ep', split_axis=0, concat_axis=0, til...  8.58 us
    all_to_all x2, starting transfers between devices, shards(): lax.all_to_all(quarter_cols, 'ep', split_axis=0, concat_axis=0, tiled=True)  7.9 us
    dot_general x2, matrix products, shards(): jnp.dot(hidden, w_down[0], preferred_element_type=jnp.float32)  5.76 us
    convert_element_type x2, other arithmetic, shards(): finished = (half_sum + partner).astype(jnp.bfloat16)  3.77 us
    dot_general x2, matrix products, pack_rows(): jnp.dot(chosen, tokens, preferred_element_type=jnp.float32)  3.03 us
    dot_general x2, matrix products, shards(): gate_val = jnp.dot(slot_rows, w_gate[0], preferred_element_type=jnp.float32)  2.95 us
  transfers between devices with their start and end apart: 6, of which 3 were waited for; matrix products, arithmetic and copies ran while one was open for 35% of the time, Pallas kernels for 0%

commit v1 on v0

--- a/solution.py
+++ b/solution.py
@@ -1,8 +1,11 @@
+import functools
 import math
 
 import jax
 import jax.numpy as jnp
 from jax import lax
+from jax.experimental import pallas as pl
+from jax.experimental.pallas import tpu as pltpu
 from jax.sharding import PartitionSpec as P
 
 QUERY_HEADS = 64
@@ -89,7 +92,7 @@
     return jnp.sum(weighted.reshape(row_count, route_count, -1), axis=1).astype(jnp.bfloat16)
 
 
-def shards(
+def sparse_shards(
     hidden_in,
     routes,
     gates,
@@ -159,6 +162,453 @@
     return (jnp.stack(attn_list), jnp.stack(moe_list))
 
 
+LANES = 128
+TILE_ROWS = 16
+PAIR = 2
+MESH = pl.DeviceIdType.MESH
+
+
+def remote(src, dst, send_sem, recv_sem, index):
+    return pltpu.make_async_remote_copy(
+        src_ref=src,
+        dst_ref=dst,
+        send_sem=send_sem,
+        recv_sem=recv_sem,
+        device_id={"ep": index},
+        device_id_type=MESH,
+    )
+
+
+def layer_kernel(
+    dims,
+    hidden_ref,
+    routes_ref,
+    gates_ref,
+    query_ref,
+    fresh_key_ref,
+    fresh_value_ref,
+    lengths_ref,
+    key_hbm,
+    value_hbm,
+    gate_hbm,
+    up_hbm,
+    down_hbm,
+    attn_ref,
+    moe_ref,
+    keys,
+    values,
+    w_gate,
+    w_up,
+    w_down,
+    gathered,
+    q_rows,
+    o_rows,
+    own_keys,
+    own_values,
+    row_weight,
+    act,
+    keep_c,
+    keep_x,
+    send_c,
+    recv_c,
+    send_x,
+    recv_x,
+    send_z,
+    recv_z,
+    load_sems,
+    gz_send,
+    gz_recv,
+    gx_send,
+    gx_recv,
+    gc_send,
+    gc_recv,
+    rc_send,
+    rc_recv,
+    rx_send,
+    rx_recv,
+    rz_send,
+    rz_recv,
+):
+    batches, rows, width, heads, kv_heads, slots, experts, depth, chunks, chunk = dims
+    ring = gz_send.shape[0]
+    block = batches * rows
+    quarter = ring * block
+    half = PAIR * quarter
+    group = heads // kv_heads
+    scale = 1.0 / math.sqrt(HEAD_SIZE)
+
+    me = lax.axis_index("ep")
+    core = lax.rem(me, PAIR)
+    across = lax.rem(me // PAIR, PAIR)
+    place = lax.rem(me, PAIR * PAIR)
+    level = me // (PAIR * PAIR)
+    mate = me + 1 - PAIR * core
+    side = me + PAIR - PAIR * PAIR * across
+
+    def up_by(step):
+        return lax.rem(level + step, ring) * (PAIR * PAIR) + place
+
+    def down_by(step):
+        return lax.rem(level + ring - step, ring) * (PAIR * PAIR) + place
+
+    loads = [
+        pltpu.make_async_copy(source, target, load_sems.at[i])
+        for i, (source, target) in enumerate(
+            (
+                (key_hbm, keys),
+                (value_hbm, values),
+                (gate_hbm, w_gate),
+                (up_hbm, w_up),
+                (down_hbm, w_down),
+            )
+        )
+    ]
+    for load in loads:
+        load.start()
+
+    barrier = pltpu.get_barrier_semaphore()
+    others = [mate, side] + [up_by(step) for step in range(1, ring)]
+    for other in others:
+        pl.semaphore_signal(barrier, inc=1, device_id={"ep": other}, device_id_type=MESH)
+
+    own = [hidden_ref[b].astype(jnp.float32) for b in range(batches)]
+    gathered[0:block, 0:width] = jnp.concatenate(own, axis=0).astype(jnp.bfloat16)
+    spread = gathered.shape[1] - width
+    lane = lax.broadcasted_iota(jnp.int32, (rows, spread), 1)
+    expert_of = lax.rem(lane, experts)
+    tails = []
+    for b in range(batches):
+        dense = jnp.zeros((rows, spread), jnp.float32)
+        for k in range(routes_ref.shape[2]):
+            named = routes_ref[b, :, k : k + 1] == expert_of
+            dense = dense + jnp.where(named, gates_ref[b, :, k : k + 1], 0.0)
+        high = dense.astype(jnp.bfloat16).astype(jnp.float32)
+        tail = jnp.where(lane < experts, high, dense - high)
+        tails.append(jnp.where(lane < 2 * experts, tail, 0.0))
+    gathered[0:block, width:] = jnp.concatenate(tails, axis=0).astype(jnp.bfloat16)
+
+    pl.semaphore_wait(barrier, len(others))
+
+    def slot(far_core, far_side, step):
+        return pl.ds(((far_core * PAIR + far_side) * ring + step) * block, block)
+
+    def gather_z(step):
+        return remote(
+            gathered.at[slot(0, 0, 0)],
+            gathered.at[slot(0, 0, step)],
+            gz_send.at[step],
+            gz_recv.at[step],
+            up_by(step),
+        )
+
+    def gather_x(step):
+        return remote(
+            gathered.at[slot(0, 0, step)],
+            gathered.at[slot(0, 1, step)],
+            gx_send.at[step],
+            gx_recv.at[step],
+            side,
+        )
+
+    def gather_c(far_side, step):
+        return remote(
+            gathered.at[slot(0, far_side, step)],
+            gathered.at[slot(1, far_side, step)],
+            gc_send.at[far_side * ring + step],
+            gc_recv.at[far_side * ring + step],
+            mate,
+        )
+
+    order = sorted(range(1, ring), key=lambda step: min(step, ring - step))
+    for step in order:
+        gather_z(step).start()
+    gather_x(0).start()
+    gather_c(0, 0).start()
+
+    for b in range(batches):
+        own_keys[b] = fresh_key_ref[b].astype(jnp.float32)
+        own_values[b] = fresh_value_ref[b].astype(jnp.float32)
+        for h in range(heads):
+            q_rows[b, h * rows : (h + 1) * rows, :] = query_ref[
+                b, :, h * HEAD_SIZE : (h + 1) * HEAD_SIZE
+            ].astype(jnp.float32)
+    loads[0].wait()
+    loads[1].wait()
+
+    head = lax.broadcasted_iota(jnp.int32, (heads, kv_heads * slots), 0)
+    column = lax.broadcasted_iota(jnp.int32, (heads, kv_heads * slots), 1)
+    position = jnp.where(head // group == column // slots, lax.rem(column, slots), slots)
+
+    def grouped(ref, b, r):
+        parts = [ref[b, pl.ds(r, 1), g * HEAD_SIZE : (g + 1) * HEAD_SIZE] for g in range(kv_heads)]
+        return jnp.concatenate(
+            [jnp.broadcast_to(part, (group, HEAD_SIZE)) for part in parts], axis=0
+        )
+
+    def stacked(ref, b, r):
+        return jnp.concatenate(
+            [ref[b, r, :, g * HEAD_SIZE : (g + 1) * HEAD_SIZE] for g in range(kv_heads)], axis=0
+        )
+
+    def attend(b, r):
+        picked = pl.ds(r, heads, stride=rows)
+        q = q_rows[b, picked, :]
+        score = lax.dot_general(
+            q.astype(jnp.bfloat16),
+            stacked(keys, b, r),
+            (((1,), (1,)), ((), ())),
+            preferred_element_type=jnp.float32,
+        )
+        score = jnp.where(position < lengths_ref[b, r], score * scale, -jnp.inf)
+        own_score = jnp.sum(q * grouped(own_keys, b, r), axis=1, keepdims=True) * scale
+        top = jnp.maximum(jnp.max(score, axis=1, keepdims=True), own_score)
+        raised = jnp.exp(score - top)
+        own_raised = jnp.exp(own_score - top)
+        total = jnp.sum(raised, axis=1, keepdims=True) + own_raised
+        probs = (raised / total).astype(jnp.bfloat16)
+        own_prob = (own_raised / total).astype(jnp.bfloat16).astype(jnp.float32)
+        out = jnp.dot(probs, stacked(values, b, r), preferred_element_type=jnp.float32)
+        o_rows[b, picked, :] = out + own_prob * grouped(own_values, b, r)
+
+    def attend_two(b, i):
+        attend(b, 2 * i)
+        attend(b, 2 * i + 1)
+
+    pairs = [(b, i) for b in range(batches) for i in range(rows // 2)]
+    forwards = [("z", step) for step in order] + [("x", step) for step in [0] + order]
+    share = -(-len(pairs) // (len(forwards) + 1))
+
+    def attend_share(turn):
+        for b, i in pairs[turn * share : (turn + 1) * share]:
+            attend_two(b, i)
+
+    attend_share(0)
+    for turn, (kind, step) in enumerate(forwards):
+        if kind == "z":
+            gather_z(step).wait_recv()
+            gather_x(step).start()
+            gather_c(0, step).start()
+        else:
+            gather_x(step).wait_recv()
+            gather_c(1, step).start()
+        attend_share(turn + 1)
+
+    expert = me // PAIR
+
+    def hidden_units(far_core):
+        span = pl.ds(far_core * half, half)
+        x = gathered[span, 0:width]
+        gate_val = jnp.dot(x, w_gate[0], preferred_element_type=jnp.float32)
+        up_val = jnp.dot(x, w_up[0], preferred_element_type=jnp.float32)
+        act[span, :] = (gate_val / (1.0 + jnp.exp(-gate_val)) * up_val).astype(jnp.bfloat16)
+        tail = gathered[span, width:].astype(jnp.float32)
+        at = lax.broadcasted_iota(jnp.int32, tail.shape, 1)
+        mine = jnp.sum(jnp.where(lax.rem(at, experts) == expert, tail, 0.0), axis=1, keepdims=True)
+        row_weight[span, :] = jnp.broadcast_to(mine, (half, LANES))
+
+    loads[2].wait()
+    loads[3].wait()
+    hidden_units(0)
+    for far_side in range(PAIR):
+        for step in range(ring):
+            gather_c(far_side, step).wait_recv()
+    hidden_units(1)
+    loads[4].wait()
+
+    def reduce_c(j):
+        return remote(send_c.at[j], recv_c.at[j], rc_send.at[j], rc_recv.at[j], mate)
+
+    def reduce_x(j):
+        return remote(send_x.at[j], recv_x.at[j], rx_send.at[j], rx_recv.at[j], side)
+
+    def reduce_z(j, step):
+        at = j * ring + step
+        return remote(
+            send_z.at[j, step], recv_z.at[j, step], rz_send.at[at], rz_recv.at[at], down_by(step)
+        )
+
+    def project(j):
+        columns = slice(j * chunk, (j + 1) * chunk)
+        for far_core in (1, 0):
+            span = pl.ds(far_core * half, half)
+            out = jnp.dot(act[span, :], w_down[0, :, columns], preferred_element_type=jnp.float32)
+            out = out * jnp.concatenate([row_weight[span, :]] * (chunk // LANES), axis=1)
+            if far_core:
+                send_c[j] = out.astype(jnp.bfloat16)
+                reduce_c(j).start()
+            else:
+                keep_c[j] = out
+
+    def after_c(j):
+        reduce_c(j).wait_recv()
+        for far_side in (1, 0):
+            span = slice(far_side * quarter, (far_side + 1) * quarter)
+            out = keep_c[j, span, :] + recv_c[j, span, :].astype(jnp.float32)
+            if far_side:
+                send_x[j] = out.astype(jnp.bfloat16)
+                reduce_x(j).start()
+            else:
+                keep_x[j] = out
+
+    def after_x(j):
+        reduce_x(j).wait_recv()
+        for step in order + [0]:
+            span = slice(step * block, (step + 1) * block)
+            out = keep_x[j, span, :] + recv_x[j, span, :].astype(jnp.float32)
+            if step:
+                send_z[j, step] = out.astype(jnp.bfloat16)
+                reduce_z(j, step).start()
+            else:
+                keep_x[j, span, :] = out
+
+    def after_z(j):
+        out = keep_x[j, 0:block, :]
+        for step in order:
+            reduce_z(j, step).wait_recv()
+            out = out + recv_z[j, step].astype(jnp.float32)
+        out = out.astype(jnp.bfloat16).astype(jnp.float32)
+        for b in range(batches):
+            moe_ref[b, :, j * chunk : (j + 1) * chunk] = out[b * rows : (b + 1) * rows].astype(
+                jnp.bfloat16
+            )
+
+    stages = (project, after_c, after_x, after_z)
+    lags = (0, 1, 2, 4)
+    for tick in range(chunks + lags[-1]):
+        for stage, lag in zip(stages, lags):
+            if 0 <= tick - lag < chunks:
+                stage(tick - lag)
+
+    for b in range(batches):
+        for h in range(heads):
+            attn_ref[b, :, h * HEAD_SIZE : (h + 1) * HEAD_SIZE] = o_rows[
+                b, h * rows : (h + 1) * rows, :
+            ].astype(jnp.bfloat16)
+
+    for step in order:
+        gather_z(step).wait_send()
+    for step in range(ring):
+        gather_x(step).wait_send()
+        for far_side in range(PAIR):
+            gather_c(far_side, step).wait_send()
+    for j in range(chunks):
+        reduce_c(j).wait_send()
+        reduce_x(j).wait_send()
+        for step in order:
+            reduce_z(j, step).wait_send()
+
+
+def dense_shards(
+    hidden_in,
+    routes,
+    gates,
+    query,
+    cached_key_rows,
+    cached_value_rows,
+    fresh_key,
+    fresh_value,
+    lengths,
+    w_gate,
+    w_up,
+    w_down,
+):
+    ep_size = lax.axis_size("ep")
+    experts = ep_size // PAIR
+    ring = ep_size // (PAIR * PAIR)
+    batches, rows, width = hidden_in.shape
+    slots = cached_key_rows.shape[2]
+    kv_heads = cached_key_rows.shape[3] // HEAD_SIZE
+    heads = query.shape[2] // HEAD_SIZE
+    depth = w_gate.shape[2]
+    chunks = 4
+    chunk = width // chunks
+    block = batches * rows
+    quarter = ring * block
+    half = PAIR * quarter
+    spread = -(-2 * experts // LANES) * LANES
+    dims = (batches, rows, width, heads, kv_heads, slots, experts, depth, chunks, chunk)
+    vmem = pl.BlockSpec(memory_space=pltpu.VMEM)
+    smem = pl.BlockSpec(memory_space=pltpu.SMEM)
+    anywhere = pl.BlockSpec(memory_space=pl.ANY)
+    bf16, f32 = jnp.bfloat16, jnp.float32
+    dma = pltpu.SemaphoreType.DMA
+    return pl.pallas_call(
+        functools.partial(layer_kernel, dims),
+        out_shape=(
+            jax.ShapeDtypeStruct(query.shape, bf16),
+            jax.ShapeDtypeStruct(hidden_in.shape, bf16),
+        ),
+        in_specs=[vmem] * 6 + [smem] + [anywhere] * 5,
+        out_specs=(vmem, vmem),
+        scratch_shapes=[
+            pltpu.VMEM(cached_key_rows.shape, bf16),
+            pltpu.VMEM(cached_value_rows.shape, bf16),
+            pltpu.VMEM(w_gate.shape, bf16),
+            pltpu.VMEM(w_up.shape, bf16),
+            pltpu.VMEM(w_down.shape, bf16),
+            pltpu.VMEM((PAIR * half, width + spread), bf16),
+            pltpu.VMEM((batches, heads * rows, HEAD_SIZE), f32),
+            pltpu.VMEM((batches, heads * rows, HEAD_SIZE), f32),
+            pltpu.VMEM(fresh_key.shape, f32),
+            pltpu.VMEM(fresh_value.shape, f32),
+            pltpu.VMEM((PAIR * half, LANES), f32),
+            pltpu.VMEM((PAIR * half, depth), bf16),
+            pltpu.VMEM((chunks, half, chunk), f32),
+            pltpu.VMEM((chunks, quarter, chunk), f32),
+            pltpu.VMEM((chunks, half, chunk), bf16),
+            pltpu.VMEM((chunks, half, chunk), bf16),
+            pltpu.VMEM((chunks, quarter, chunk), bf16),
+            pltpu.VMEM((chunks, quarter, chunk), bf16),
+            pltpu.VMEM((chunks, ring, block, chunk), bf16),
+            pltpu.VMEM((chunks, ring, block, chunk), bf16),
+            dma((5,)),
+            dma((ring,)),
+            dma((ring,)),
+            dma((ring,)),
+            dma((ring,)),
+            dma((PAIR * ring,)),
+            dma((PAIR * ring,)),
+            dma((chunks,)),
+            dma((chunks,)),
+            dma((chunks,)),
+            dma((chunks,)),
+            dma((chunks * ring,)),
+            dma((chunks * ring,)),
+        ],
+        compiler_params=pltpu.CompilerParams(
+            collective_id=0, has_side_effects=True, vmem_limit_bytes=40 * 1024 * 1024
+        ),
+        cost_estimate=pl.CostEstimate(
+            flops=6 * PAIR * half * width * depth, bytes_accessed=8 * 1024 * 1024, transcendentals=0
+        ),
+    )(
+        hidden_in,
+        routes,
+        gates,
+        query,
+        fresh_key,
+        fresh_value,
+        lengths,
+        cached_key_rows,
+        cached_value_rows,
+        w_gate,
+        w_up,
+        w_down,
+    )
+
+
+def shards(*args):
+    hidden_in, routes = args[0], args[1]
+    ep_size = lax.axis_size("ep")
+    batches, rows, width = hidden_in.shape
+    every_expert = routes.shape[2] == ep_size // PAIR
+    fits = ep_size % (PAIR * PAIR) == 0 and ep_size > PAIR * PAIR and lax.axis_size("tp") == 1
+    tiles = batches * rows % TILE_ROWS == 0 and rows % 8 == 0 and width % (4 * LANES) == 0
+    if every_expert and fits and tiles:
+        return dense_shards(*args)
+    return sparse_shards(*args)
+
+
 def solution(mesh):
     in_specs = (
         P(None, ("grp", "ep"), None),

time: 87.3 us -> 48.8 us (0.56)
  Pallas kernels: 0 us -> 34.3 us
  waiting for transfers between devices: 25.1 us -> 0 us
  starting transfers between devices: 21.8 us -> 0 us
  matrix products: 13.5 us -> 0 us
  other arithmetic: 10.9 us -> 0 us
    pallas_call x0 -> x1, Pallas kernels: none -> 34.3 us  [dense_shards(): pl.pallas_call(functools.partial(layer_kernel, dims), out_shape=(jax.Shap...]
    all_to_all x4 -> x0, waiting for transfers between devices: 25 us -> none  [the longest x2 16.5 us: shards(): lax.all_to_all(quarter_cols, 'ep', split_axis=0, concat_axis=0, tiled=True)]
    all_to_all x4 -> x0, starting transfers between devices: 21.3 us -> none  [the longest x2 13.4 us: shards(): lax.all_to_all(buffers[batch_idx], 'ep', split_axis=0, concat_axis=0, til...]
    dot_general x12 -> x0, matrix products: 13.5 us -> none  [the longest x2 5.76 us: shards(): jnp.dot(hidden, w_down[0], preferred_element_type=jnp.float32)]
    unnamed x39 -> x26, local copies, waits for them, and re-layouts: 0.92 us -> 13.3 us
    slice x7 -> x0, local copies, waits for them, and re-layouts: 5.05 us -> none  [the longest x1 2.13 us: shards(): cached_key_rows[batch_idx]]
    convert_element_type x7 -> x0, other arithmetic: 4.36 us -> none  [the longest x2 3.77 us: shards(): finished = (half_sum + partner).astype(jnp.bfloat16)]
    gather x4 -> x0, local copies, waits for them, and re-layouts: 2.83 us -> none  [the longest x2 1.42 us: combine_rows(): lower = jnp.take(flat_back, first_slot, axis=0)]
  transfers between devices with their start and end apart: 6 -> 0, of which waited for: 3 -> 0; matrix products, arithmetic and copies ran while one was open for 35% -> 0% of each run, Pallas kernels for 0% -> 0%
where the time goes in v1:
time: 48.8 us; the launch traced here: 48.3 us
  Pallas kernels  34.3 us (70%)
  local copies, waits for them, and re-layouts  13.3 us (27%)
  between operations  0.66 us (1%)
    pallas_call x1, Pallas kernels, dense_shards(): pl.pallas_call(functools.partial(layer_kernel, dims), out_shape=(jax.Shap...  34.3 us
    unnamed x26, local copies, waits for them, and re-layouts  13.3 us

profile of v1, /device:TPU:0, one launch (start us, length us, event | category | flops | bytes accessed | tf_op | source)
XLA Modules:
  0.0 48.3 jit_solution(10451540901314444632)
XLA Ops:
  0.6 0.0 copy-start
  0.6 1.4 %copy-done = bf16[1,2048,384]{2,1,0:T(8,128)(2,1)S(1)} copy-done((bf16[1,2048,384]{2,1,0:T(8,128)(2,1)S(1)}, bf16[1,2048,384]{2,1,0:T(8,128)(2,1)}, u32[]{:S(2)}) %copy-start) | copy-done | bytes 1572888
  2.0 0.0 copy-start.1
  2.0 1.4 %copy-done.1 = bf16[1,2048,384]{2,1,0:T(8,128)(2,1)S(1)} copy-done((bf16[1,2048,384]{2,1,0:T(8,128)(2,1)S(1)}, bf16[1,2048,384]{2,1,0:T(8,128)(2,1)}, u32[]{:S(2)}) %copy-start.1) | copy-done | bytes 1572888
  3.5 0.0 copy-start.2
  3.5 1.4 %copy-done.2 = bf16[1,384,2048]{2,1,0:T(8,128)(2,1)S(1)} copy-done((bf16[1,384,2048]{2,1,0:T(8,128)(2,1)S(1)}, bf16[1,384,2048]{2,1,0:T(8,128)(2,1)}, u32[]{:S(2)}) %copy-start.2) | copy-done | bytes 1572888
  4.9 0.0 copy-start.3
  4.9 1.2 %copy-done.3 = bf16[2,8,64,512]{3,2,1,0:T(8,128)(2,1)S(1)} copy-done((bf16[2,8,64,512]{3,2,1,0:T(8,128)(2,1)S(1)}, bf16[2,8,64,512]{3,2,1,0:T(8,128)(2,1)}, u32[]{:S(2)}) %copy-start.3) | copy-done | bytes 1048600
  6.1 0.0 copy-start.4
  6.1 1.2 %copy-done.4 = bf16[2,8,64,512]{3,2,1,0:T(8,128)(2,1)S(1)} copy-done((bf16[2,8,64,512]{3,2,1,0:T(8,128)(2,1)S(1)}, bf16[2,8,64,512]{3,2,1,0:T(8,128)(2,1)}, u32[]{:S(2)}) %copy-start.4) | copy-done | bytes 1048600
  7.3 0.0 copy-start.5
  7.3 0.9 %copy-done.5 = bf16[2,8,8192]{2,1,0:T(8,128)(2,1)S(1)} copy-done((bf16[2,8,8192]{2,1,0:T(8,128)(2,1)S(1)}, bf16[2,8,8192]{2,1,0:T(8,128)(2,1)}, u32[]{:S(2)}) %copy-start.5) | copy-done | bytes 262168
  8.3 0.0 copy-start.6
  8.3 0.8 %copy-done.6 = bf16[2,8,2048]{2,1,0:T(8,128)(2,1)S(1)} copy-done((bf16[2,8,2048]{2,1,0:T(8,128)(2,1)S(1)}, bf16[2,8,2048]{2,1,0:T(8,128)(2,1)}, u32[]{:S(2)}) %copy-start.6) | copy-done | bytes 65560
  9.1 0.0 copy-start.7
  9.1 0.7 %copy-done.7 = bf16[2,8,512]{2,1,0:T(8,128)(2,1)S(1)} copy-done((bf16[2,8,512]{2,1,0:T(8,128)(2,1)S(1)}, bf16[2,8,512]{2,1,0:T(8,128)(2,1)}, u32[]{:S(2)}) %copy-start.7) | copy-done | bytes 16408
  9.8 0.0 copy-start.8
  9.8 0.7 %copy-done.8 = bf16[2,8,512]{2,1,0:T(8,128)(2,1)S(1)} copy-done((bf16[2,8,512]{2,1,0:T(8,128)(2,1)S(1)}, bf16[2,8,512]{2,1,0:T(8,128)(2,1)}, u32[]{:S(2)}) %copy-start.8) | copy-done | bytes 16408
  10.5 0.0 copy-start.9
  10.5 0.7 %copy-done.9 = s32[2,8,8]{2,1,0:T(8,128)S(1)} copy-done((s32[2,8,8]{2,1,0:T(8,128)S(1)}, s32[2,8,8]{2,1,0:T(8,128)}, u32[]{:S(2)}) %copy-start.9) | copy-done | bytes 536
  11.2 0.0 copy-start.10
  11.2 0.7 %copy-done.10 = f32[2,8,8]{2,1,0:T(8,128)S(1)} copy-done((f32[2,8,8]{2,1,0:T(8,128)S(1)}, f32[2,8,8]{2,1,0:T(8,128)}, u32[]{:S(2)}) %copy-start.10) | copy-done | bytes 536
  11.9 0.0 copy-start.11
  11.9 0.7 %copy-done.11 = s32[2,8]{1,0:T(2,128)S(1)} copy-done((s32[2,8]{1,0:T(2,128)S(1)}, s32[2,8]{1,0:T(2,128)}, u32[]{:S(2)}) %copy-start.11) | copy-done | bytes 88
  12.6 34.3 %shard_map.131 = (bf16[2,8,8192]{2,1,0:T(8,128)(2,1)S(1)}, bf16[2,8,2048]{2,1,0:T(8,128)(2,1)S(1)}) custom-call(bf16[2,8,2048]{2,1,0:T(8,128)(2,1)S(1)} %copy-done.6, s32[2,8,8]{2,1,0:T(8,128)S(1)} %copy-done.9, f32[2,8,8]{2,1,0:T(8,128)S(1)} %copy-done.10, bf16[2,8,8192]{2,1,0:T(8,128)(2,1)S(1)} %copy-done.5, bf16[2,8,512]{2,1,0:T(8,128)(2,1)S(1)} %copy-done.7, ...), custom_call_target="tpu_custom_call" | custom-call | flops 1207959552 | bytes 8388608 | tf_op jit(solution)/shard_map/pallas_call | solution.py:535
  46.9 0.7 %copy.16 = bf16[2,8,8192]{2,1,0:T(8,128)(2,1)} copy(bf16[2,8,8192]{2,1,0:T(8,128)(2,1)S(1)} %get-tuple-element.4) | data formatting | bytes 524288
  47.6 0.6 %copy.17 = bf16[2,8,2048]{2,1,0:T(8,128)(2,1)} copy(bf16[2,8,2048]{2,1,0:T(8,128)(2,1)S(1)} %get-tuple-element.5) | data formatting | bytes 131072
Async XLA Ops:
  0.6 1.4 %copy-start = (bf16[1,2048,384]{2,1,0:T(8,128)(2,1)S(1)}, bf16[1,2048,384]{2,1,0:T(8,128)(2,1)}, u32[]{:S(2)}) copy-start(bf16[1,2048,384]{2,1,0:T(8,128)(2,1)} %gate_hbm.1) | copy-start | bytes 4718596
  2.0 1.4 %copy-start.1 = (bf16[1,2048,384]{2,1,0:T(8,128)(2,1)S(1)}, bf16[1,2048,384]{2,1,0:T(8,128)(2,1)}, u32[]{:S(2)}) copy-start(bf16[1,2048,384]{2,1,0:T(8,128)(2,1)} %up_hbm.1) | copy-start | bytes 4718596
  3.5 1.4 %copy-start.2 = (bf16[1,384,2048]{2,1,0:T(8,128)(2,1)S(1)}, bf16[1,384,2048]{2,1,0:T(8,128)(2,1)}, u32[]{:S(2)}) copy-start(bf16[1,384,2048]{2,1,0:T(8,128)(2,1)} %down_hbm.1) | copy-start | bytes 4718596
  4.9 1.2 %copy-start.3 = (bf16[2,8,64,512]{3,2,1,0:T(8,128)(2,1)S(1)}, bf16[2,8,64,512]{3,2,1,0:T(8,128)(2,1)}, u32[]{:S(2)}) copy-start(bf16[2,8,64,512]{3,2,1,0:T(8,128)(2,1)} %key_hbm.1) | copy-start | bytes 3145732
  6.1 1.2 %copy-start.4 = (bf16[2,8,64,512]{3,2,1,0:T(8,128)(2,1)S(1)}, bf16[2,8,64,512]{3,2,1,0:T(8,128)(2,1)}, u32[]{:S(2)}) copy-start(bf16[2,8,64,512]{3,2,1,0:T(8,128)(2,1)} %value_hbm.1) | copy-start | bytes 3145732
  7.3 0.9 %copy-start.5 = (bf16[2,8,8192]{2,1,0:T(8,128)(2,1)S(1)}, bf16[2,8,8192]{2,1,0:T(8,128)(2,1)}, u32[]{:S(2)}) copy-start(bf16[2,8,8192]{2,1,0:T(8,128)(2,1)} %query_ref.1) | copy-start | bytes 786436
  8.3 0.8 %copy-start.6 = (bf16[2,8,2048]{2,1,0:T(8,128)(2,1)S(1)}, bf16[2,8,2048]{2,1,0:T(8,128)(2,1)}, u32[]{:S(2)}) copy-start(bf16[2,8,2048]{2,1,0:T(8,128)(2,1)} %hidden_ref.1) | copy-start | bytes 196612
  9.1 0.7 %copy-start.7 = (bf16[2,8,512]{2,1,0:T(8,128)(2,1)S(1)}, bf16[2,8,512]{2,1,0:T(8,128)(2,1)}, u32[]{:S(2)}) copy-start(bf16[2,8,512]{2,1,0:T(8,128)(2,1)} %fresh_key_ref.1) | copy-start | bytes 49156
  9.8 0.7 %copy-start.8 = (bf16[2,8,512]{2,1,0:T(8,128)(2,1)S(1)}, bf16[2,8,512]{2,1,0:T(8,128)(2,1)}, u32[]{:S(2)}) copy-start(bf16[2,8,512]{2,1,0:T(8,128)(2,1)} %fresh_value_ref.1) | copy-start | bytes 49156
  10.5 0.7 %copy-start.9 = (s32[2,8,8]{2,1,0:T(8,128)S(1)}, s32[2,8,8]{2,1,0:T(8,128)}, u32[]{:S(2)}) copy-start(s32[2,8,8]{2,1,0:T(8,128)} %routes_ref.1) | copy-start | bytes 1540
  11.2 0.7 %copy-start.10 = (f32[2,8,8]{2,1,0:T(8,128)S(1)}, f32[2,8,8]{2,1,0:T(8,128)}, u32[]{:S(2)}) copy-start(f32[2,8,8]{2,1,0:T(8,128)} %gates_ref.1) | copy-start | bytes 1540
  11.9 0.7 %copy-start.11 = (s32[2,8]{1,0:T(2,128)S(1)}, s32[2,8]{1,0:T(2,128)}, u32[]{:S(2)}) copy-start(s32[2,8]{1,0:T(2,128)} %lengths_ref.1) | copy-start | bytes 196

commit v2 on v1

--- a/solution.py
+++ b/solution.py
@@ -181,13 +181,13 @@
 
 def layer_kernel(
     dims,
-    hidden_ref,
-    routes_ref,
-    gates_ref,
-    query_ref,
-    fresh_key_ref,
-    fresh_value_ref,
     lengths_ref,
+    hidden_hbm,
+    routes_hbm,
+    gates_hbm,
+    query_hbm,
+    fresh_key_hbm,
+    fresh_value_hbm,
     key_hbm,
     value_hbm,
     gate_hbm,
@@ -195,6 +195,12 @@
     down_hbm,
     attn_ref,
     moe_ref,
+    hidden_ref,
+    routes_ref,
+    gates_ref,
+    query_ref,
+    fresh_key_ref,
+    fresh_value_ref,
     keys,
     values,
     w_gate,
@@ -255,6 +261,12 @@
         pltpu.make_async_copy(source, target, load_sems.at[i])
         for i, (source, target) in enumerate(
             (
+                (hidden_hbm, hidden_ref),
+                (routes_hbm, routes_ref),
+                (gates_hbm, gates_ref),
+                (query_hbm, query_ref),
+                (fresh_key_hbm, fresh_key_ref),
+                (fresh_value_hbm, fresh_value_ref),
                 (key_hbm, keys),
                 (value_hbm, values),
                 (gate_hbm, w_gate),
@@ -271,8 +283,9 @@
     for other in others:
         pl.semaphore_signal(barrier, inc=1, device_id={"ep": other}, device_id_type=MESH)
 
-    own = [hidden_ref[b].astype(jnp.float32) for b in range(batches)]
-    gathered[0:block, 0:width] = jnp.concatenate(own, axis=0).astype(jnp.bfloat16)
+    for load in loads[0:3]:
+        load.wait()
+    gathered[0:block, 0:width] = hidden_ref[...]
     spread = gathered.shape[1] - width
     lane = lax.broadcasted_iota(jnp.int32, (rows, spread), 1)
     expert_of = lax.rem(lane, experts)
@@ -325,22 +338,21 @@
     gather_x(0).start()
     gather_c(0, 0).start()
 
-    for b in range(batches):
-        own_keys[b] = fresh_key_ref[b].astype(jnp.float32)
-        own_values[b] = fresh_value_ref[b].astype(jnp.float32)
-        for h in range(heads):
-            q_rows[b, h * rows : (h + 1) * rows, :] = query_ref[
-                b, :, h * HEAD_SIZE : (h + 1) * HEAD_SIZE
-            ].astype(jnp.float32)
-    loads[0].wait()
-    loads[1].wait()
+    for load in loads[3:8]:
+        load.wait()
+    own_keys[...] = fresh_key_ref[...].astype(jnp.float32)
+    own_values[...] = fresh_value_ref[...].astype(jnp.float32)
+    for h in range(heads):
+        q_rows[h * block : (h + 1) * block, :] = query_ref[
+            :, h * HEAD_SIZE : (h + 1) * HEAD_SIZE
+        ].astype(jnp.float32)
 
     head = lax.broadcasted_iota(jnp.int32, (heads, kv_heads * slots), 0)
     column = lax.broadcasted_iota(jnp.int32, (heads, kv_heads * slots), 1)
     position = jnp.where(head // group == column // slots, lax.rem(column, slots), slots)
 
-    def grouped(ref, b, r):
-        parts = [ref[b, pl.ds(r, 1), g * HEAD_SIZE : (g + 1) * HEAD_SIZE] for g in range(kv_heads)]
+    def grouped(ref, row):
+        parts = [ref[row : row + 1, g * HEAD_SIZE : (g + 1) * HEAD_SIZE] for g in range(kv_heads)]
         return jnp.concatenate(
             [jnp.broadcast_to(part, (group, HEAD_SIZE)) for part in parts], axis=0
         )
@@ -350,9 +362,10 @@
             [ref[b, r, :, g * HEAD_SIZE : (g + 1) * HEAD_SIZE] for g in range(kv_heads)], axis=0
         )
 
-    def attend(b, r):
-        picked = pl.ds(r, heads, stride=rows)
-        q = q_rows[b, picked, :]
+    def attend(row):
+        b, r = divmod(row, rows)
+        picked = pl.ds(row, heads, stride=block)
+        q = q_rows[picked, :]
         score = lax.dot_general(
             q.astype(jnp.bfloat16),
             stacked(keys, b, r),
@@ -360,38 +373,32 @@
             preferred_element_type=jnp.float32,
         )
         score = jnp.where(position < lengths_ref[b, r], score * scale, -jnp.inf)
-        own_score = jnp.sum(q * grouped(own_keys, b, r), axis=1, keepdims=True) * scale
+        own_score = jnp.sum(q * grouped(own_keys, row), axis=1, keepdims=True) * scale
         top = jnp.maximum(jnp.max(score, axis=1, keepdims=True), own_score)
         raised = jnp.exp(score - top)
         own_raised = jnp.exp(own_score - top)
-        total = jnp.sum(raised, axis=1, keepdims=True) + own_raised
-        probs = (raised / total).astype(jnp.bfloat16)
-        own_prob = (own_raised / total).astype(jnp.bfloat16).astype(jnp.float32)
+        share = 1.0 / (jnp.sum(raised, axis=1, keepdims=True) + own_raised)
+        probs = (raised * share).astype(jnp.bfloat16)
+        own_prob = (own_raised * share).astype(jnp.bfloat16).astype(jnp.float32)
         out = jnp.dot(probs, stacked(values, b, r), preferred_element_type=jnp.float32)
-        o_rows[b, picked, :] = out + own_prob * grouped(own_values, b, r)
-
-    def attend_two(b, i):
-        attend(b, 2 * i)
-        attend(b, 2 * i + 1)
-
-    pairs = [(b, i) for b in range(batches) for i in range(rows // 2)]
-    forwards = [("z", step) for step in order] + [("x", step) for step in [0] + order]
-    share = -(-len(pairs) // (len(forwards) + 1))
-
-    def attend_share(turn):
-        for b, i in pairs[turn * share : (turn + 1) * share]:
-            attend_two(b, i)
-
-    attend_share(0)
-    for turn, (kind, step) in enumerate(forwards):
-        if kind == "z":
-            gather_z(step).wait_recv()
-            gather_x(step).start()
-            gather_c(0, step).start()
-        else:
-            gather_x(step).wait_recv()
-            gather_c(1, step).start()
-        attend_share(turn + 1)
+        o_rows[picked, :] = out + own_prob * grouped(own_values, row)
+
+    todo = list(range(block))
+
+    def attend_some(count):
+        for _ in range(min(count, len(todo))):
+            attend(todo.pop(0))
+
+    attend_some(2)
+    for step in order:
+        gather_z(step).wait_recv()
+        gather_x(step).start()
+        gather_c(0, step).start()
+        attend_some(1)
+    for step in [0] + order:
+        gather_x(step).wait_recv()
+        gather_c(1, step).start()
+        attend_some(1)
 
     expert = me // PAIR
 
@@ -406,14 +413,14 @@
         mine = jnp.sum(jnp.where(lax.rem(at, experts) == expert, tail, 0.0), axis=1, keepdims=True)
         row_weight[span, :] = jnp.broadcast_to(mine, (half, LANES))
 
-    loads[2].wait()
-    loads[3].wait()
+    loads[8].wait()
+    loads[9].wait()
     hidden_units(0)
     for far_side in range(PAIR):
         for step in range(ring):
             gather_c(far_side, step).wait_recv()
     hidden_units(1)
-    loads[4].wait()
+    loads[10].wait()
 
     def reduce_c(j):
         return remote(send_c.at[j], recv_c.at[j], rc_send.at[j], rc_recv.at[j], mate)
@@ -466,24 +473,24 @@
         for step in order:
             reduce_z(j, step).wait_recv()
             out = out + recv_z[j, step].astype(jnp.float32)
-        out = out.astype(jnp.bfloat16).astype(jnp.float32)
-        for b in range(batches):
-            moe_ref[b, :, j * chunk : (j + 1) * chunk] = out[b * rows : (b + 1) * rows].astype(
-                jnp.bfloat16
-            )
-
-    stages = (project, after_c, after_x, after_z)
-    lags = (0, 1, 2, 4)
-    for tick in range(chunks + lags[-1]):
-        for stage, lag in zip(stages, lags):
-            if 0 <= tick - lag < chunks:
-                stage(tick - lag)
-
-    for b in range(batches):
-        for h in range(heads):
-            attn_ref[b, :, h * HEAD_SIZE : (h + 1) * HEAD_SIZE] = o_rows[
-                b, h * rows : (h + 1) * rows, :
-            ].astype(jnp.bfloat16)
+        moe_ref[:, j * chunk : (j + 1) * chunk] = out.astype(jnp.bfloat16)
+
+    for tick in range(chunks + 2):
+        if tick < chunks:
+            project(tick)
+        if tick >= 2:
+            after_c(tick - 2)
+    attend_some(2)
+    for j in range(chunks):
+        after_x(j)
+        attend_some(1)
+    attend_some(block)
+    for h in range(heads):
+        attn_ref[:, h * HEAD_SIZE : (h + 1) * HEAD_SIZE] = o_rows[
+            h * block : (h + 1) * block, :
+        ].astype(jnp.bfloat16)
+    for j in range(chunks):
+        after_z(j)
 
     for step in order:
         gather_z(step).wait_send()
@@ -520,7 +527,7 @@
     kv_heads = cached_key_rows.shape[3] // HEAD_SIZE
     heads = query.shape[2] // HEAD_SIZE
     depth = w_gate.shape[2]
-    chunks = 4
+    chunks = 8
     chunk = width // chunks
     block = batches * rows
     quarter = ring * block
@@ -532,25 +539,34 @@
     anywhere = pl.BlockSpec(memory_space=pl.ANY)
     bf16, f32 = jnp.bfloat16, jnp.float32
     dma = pltpu.SemaphoreType.DMA
-    return pl.pallas_call(
+    def flat(array):
+        return array.reshape(block, array.shape[2])
+
+    attn_out, moe_out = pl.pallas_call(
         functools.partial(layer_kernel, dims),
         out_shape=(
-            jax.ShapeDtypeStruct(query.shape, bf16),
-            jax.ShapeDtypeStruct(hidden_in.shape, bf16),
+            jax.ShapeDtypeStruct((block, query.shape[2]), bf16),
+            jax.ShapeDtypeStruct((block, width), bf16),
         ),
-        in_specs=[vmem] * 6 + [smem] + [anywhere] * 5,
+        in_specs=[smem] + [anywhere] * 11,
         out_specs=(vmem, vmem),
         scratch_shapes=[
+            pltpu.VMEM((block, width), bf16),
+            pltpu.VMEM(routes.shape, jnp.int32),
+            pltpu.VMEM(gates.shape, f32),
+            pltpu.VMEM((block, query.shape[2]), bf16),
+            pltpu.VMEM((block, fresh_key.shape[2]), bf16),
+            pltpu.VMEM((block, fresh_value.shape[2]), bf16),
             pltpu.VMEM(cached_key_rows.shape, bf16),
             pltpu.VMEM(cached_value_rows.shape, bf16),
             pltpu.VMEM(w_gate.shape, bf16),
             pltpu.VMEM(w_up.shape, bf16),
             pltpu.VMEM(w_down.shape, bf16),
             pltpu.VMEM((PAIR * half, width + spread), bf16),
-            pltpu.VMEM((batches, heads * rows, HEAD_SIZE), f32),
-            pltpu.VMEM((batches, heads * rows, HEAD_SIZE), f32),
-            pltpu.VMEM(fresh_key.shape, f32),
-            pltpu.VMEM(fresh_value.shape, f32),
+            pltpu.VMEM((heads * block, HEAD_SIZE), f32),
+            pltpu.VMEM((heads * block, HEAD_SIZE), f32),
+            pltpu.VMEM((block, fresh_key.shape[2]), f32),
+            pltpu.VMEM((block, fresh_value.shape[2]), f32),
             pltpu.VMEM((PAIR * half, LANES), f32),
             pltpu.VMEM((PAIR * half, depth), bf16),
             pltpu.VMEM((chunks, half, chunk), f32),
@@ -561,7 +577,7 @@
             pltpu.VMEM((chunks, quarter, chunk), bf16),
             pltpu.VMEM((chunks, ring, block, chunk), bf16),
             pltpu.VMEM((chunks, ring, block, chunk), bf16),
-            dma((5,)),
+            dma((11,)),
             dma((ring,)),
             dma((ring,)),
             dma((ring,)),
@@ -576,25 +592,26 @@
             dma((chunks * ring,)),
         ],
         compiler_params=pltpu.CompilerParams(
-            collective_id=0, has_side_effects=True, vmem_limit_bytes=40 * 1024 * 1024
+            collective_id=0, has_side_effects=True, vmem_limit_bytes=63 * 1024 * 1024
         ),
         cost_estimate=pl.CostEstimate(
             flops=6 * PAIR * half * width * depth, bytes_accessed=8 * 1024 * 1024, transcendentals=0
         ),
     )(
-        hidden_in,
+        lengths,
+        flat(hidden_in),
         routes,
         gates,
-        query,
-        fresh_key,
-        fresh_value,
-        lengths,
+        flat(query),
+        flat(fresh_key),
+        flat(fresh_value),
         cached_key_rows,
         cached_value_rows,
         w_gate,
         w_up,
         w_down,
     )
+    return attn_out.reshape(query.shape), moe_out.reshape(hidden_in.shape)
 
 
 def shards(*args):
@@ -603,7 +620,7 @@
     batches, rows, width = hidden_in.shape
     every_expert = routes.shape[2] == ep_size // PAIR
     fits = ep_size % (PAIR * PAIR) == 0 and ep_size > PAIR * PAIR and lax.axis_size("tp") == 1
-    tiles = batches * rows % TILE_ROWS == 0 and rows % 8 == 0 and width % (4 * LANES) == 0
+    tiles = batches * rows % TILE_ROWS == 0 and rows % 8 == 0 and width % (8 * LANES) == 0
     if every_expert and fits and tiles:
         return dense_shards(*args)
     return sparse_shards(*args)

time: 48.8 us -> 37.3 us (0.76)
  local copies, waits for them, and re-layouts: 13.3 us -> 3.14 us
  Pallas kernels: 34.3 us -> 33.3 us
    unnamed x26 -> x2, local copies, waits for them, and re-layouts: 13.3 us -> 3.14 us
    pallas_call x1, Pallas kernels: 34.3 us -> 33.3 us  [dense_shards(): pl.pallas_call(functools.partial(layer_kernel, dims), out_shape=(jax.Shap...]
where the time goes in v2:
time: 37.3 us; the launch traced here: 37.1 us
  Pallas kernels  33.3 us (89%)
  local copies, waits for them, and re-layouts  3.14 us (8%)
  between operations  0.64 us (2%)
    pallas_call x1, Pallas kernels, dense_shards(): pl.pallas_call(functools.partial(layer_kernel, dims), out_shape=(jax.Shap...  33.3 us
    unnamed x2, local copies, waits for them, and re-layouts  3.14 us

profile of v2, /device:TPU:0, one launch (start us, length us, event | category | flops | bytes accessed | tf_op | source)
XLA Modules:
  0.0 37.1 jit_solution(4816848306204967708)
XLA Ops:
  0.6 33.3 %shard_map.131 = (bf16[16,8192]{1,0:T(8,128)(2,1)}, bf16[16,2048]{1,0:T(8,128)(2,1)}) custom-call(s32[2,8]{1,0:T(2,128)} %lengths_ref.1, bf16[16,2048]{1,0:T(8,128)(2,1)} %bitcast.8, s32[2,8,8]{2,1,0:T(8,128)} %routes_hbm.1, f32[2,8,8]{2,1,0:T(8,128)} %gates_hbm.1, bf16[16,8192]{1,0:T(8,128)(2,1)} %bitcast.7, bf16[16,512]{1,0:T(8,128)(2,1)} %bitcast.10, ...), custom_call_target="tpu_custom_call" | custom-call | flops 1207959552 | bytes 8388608 | tf_op jit(solution)/shard_map/pallas_call | solution.py:545
  34.0 1.7 %copy.16 = bf16[2,8,8192]{2,1,0:T(8,128)(2,1)} copy(bf16[2,8,8192]{2,1,0:T(8,128)(2,1)} %bitcast.6) | data formatting | bytes 524288
  35.6 1.5 %copy.17 = bf16[2,8,2048]{2,1,0:T(8,128)(2,1)} copy(bf16[2,8,2048]{2,1,0:T(8,128)(2,1)} %bitcast.9) | data formatting | bytes 131072

commit v3 on v2

--- a/solution.py
+++ b/solution.py
@@ -193,6 +193,8 @@
     gate_hbm,
     up_hbm,
     down_hbm,
+    attn_hbm,
+    moe_hbm,
     attn_ref,
     moe_ref,
     hidden_ref,
@@ -254,6 +256,14 @@
     def up_by(step):
         return lax.rem(level + step, ring) * (PAIR * PAIR) + place
 
+    shorter = jnp.minimum(level, ring - 1 - level)
+    longer = 1 - 2 * (level // ((ring + 1) // 2))
+
+    def nearest(turn):
+        distance = jnp.where(turn <= 2 * shorter, (turn + 1) // 2, turn - shorter)
+        towards = jnp.where(turn <= 2 * shorter, (2 * (turn % 2) - 1) * longer, longer)
+        return lax.rem(distance * towards + ring, ring)
+
     def down_by(step):
         return lax.rem(level + ring - step, ring) * (PAIR * PAIR) + place
 
@@ -303,7 +313,8 @@
     pl.semaphore_wait(barrier, len(others))
 
     def slot(far_core, far_side, step):
-        return pl.ds(((far_core * PAIR + far_side) * ring + step) * block, block)
+        start = ((far_core * PAIR + far_side) * ring + step) * block
+        return pl.ds(pl.multiple_of(start, block), block)
 
     def gather_z(step):
         return remote(
@@ -332,8 +343,10 @@
             mate,
         )
 
-    order = sorted(range(1, ring), key=lambda step: min(step, ring - step))
-    for step in order:
+    order = list(range(1, ring))
+    to_near = [nearest(turn) for turn in order]
+    from_near = [lax.rem(ring - step, ring) for step in to_near]
+    for step in to_near:
         gather_z(step).start()
     gather_x(0).start()
     gather_c(0, 0).start()
@@ -389,16 +402,16 @@
         for _ in range(min(count, len(todo))):
             attend(todo.pop(0))
 
-    attend_some(2)
-    for step in order:
+    for step in from_near:
         gather_z(step).wait_recv()
         gather_x(step).start()
         gather_c(0, step).start()
-        attend_some(1)
-    for step in [0] + order:
+        attend_some(2)
+    for turn, step in enumerate([0] + from_near):
         gather_x(step).wait_recv()
         gather_c(1, step).start()
-        attend_some(1)
+        if turn % 2:
+            attend_some(2)
 
     expert = me // PAIR
 
@@ -483,14 +496,19 @@
     attend_some(2)
     for j in range(chunks):
         after_x(j)
-        attend_some(1)
+        if j % 2 == 0:
+            attend_some(2)
     attend_some(block)
     for h in range(heads):
         attn_ref[:, h * HEAD_SIZE : (h + 1) * HEAD_SIZE] = o_rows[
             h * block : (h + 1) * block, :
         ].astype(jnp.bfloat16)
+    store_attn = pltpu.make_async_copy(attn_ref, attn_hbm, load_sems.at[11])
+    store_attn.start()
     for j in range(chunks):
         after_z(j)
+    store_moe = pltpu.make_async_copy(moe_ref, moe_hbm, load_sems.at[12])
+    store_moe.start()
 
     for step in order:
         gather_z(step).wait_send()
@@ -503,6 +521,38 @@
         reduce_x(j).wait_send()
         for step in order:
             reduce_z(j, step).wait_send()
+    store_attn.wait()
+    store_moe.wait()
+
+
+def finish_kernel(attn_in, moe_in, attn_out, moe_out, sems):
+    copies = [pltpu.make_async_copy(moe_in, moe_out, sems.at[0])]
+    pieces = sems.shape[0] - 1
+    size = attn_in.shape[1] // pieces
+    for i in range(pieces):
+        span = pl.ds(i * size, size)
+        copies.append(
+            pltpu.make_async_copy(attn_in.at[:, span], attn_out.at[:, span], sems.at[1 + i])
+        )
+    for copy in copies:
+        copy.start()
+    for copy in copies:
+        copy.wait()
+
+
+def finished(attn_out, moe_out):
+    hbm = pl.BlockSpec(memory_space=pl.ANY)
+    return pl.pallas_call(
+        finish_kernel,
+        out_shape=(
+            jax.ShapeDtypeStruct(attn_out.shape, attn_out.dtype),
+            jax.ShapeDtypeStruct(moe_out.shape, moe_out.dtype),
+        ),
+        in_specs=[hbm, hbm],
+        out_specs=(hbm, hbm),
+        scratch_shapes=[pltpu.SemaphoreType.DMA((5,))],
+        compiler_params=pltpu.CompilerParams(vmem_limit_bytes=63 * 1024 * 1024),
+    )(attn_out, moe_out)
 
 
 def dense_shards(
@@ -534,9 +584,8 @@
     half = PAIR * quarter
     spread = -(-2 * experts // LANES) * LANES
     dims = (batches, rows, width, heads, kv_heads, slots, experts, depth, chunks, chunk)
-    vmem = pl.BlockSpec(memory_space=pltpu.VMEM)
     smem = pl.BlockSpec(memory_space=pltpu.SMEM)
-    anywhere = pl.BlockSpec(memory_space=pl.ANY)
+    hbm = pl.BlockSpec(memory_space=pl.ANY)
     bf16, f32 = jnp.bfloat16, jnp.float32
     dma = pltpu.SemaphoreType.DMA
     def flat(array):
@@ -548,9 +597,11 @@
             jax.ShapeDtypeStruct((block, query.shape[2]), bf16),
             jax.ShapeDtypeStruct((block, width), bf16),
         ),
-        in_specs=[smem] + [anywhere] * 11,
-        out_specs=(vmem, vmem),
+        in_specs=[smem] + [hbm] * 11,
+        out_specs=(hbm, hbm),
         scratch_shapes=[
+            pltpu.VMEM((block, query.shape[2]), bf16),
+            pltpu.VMEM((block, width), bf16),
             pltpu.VMEM((block, width), bf16),
             pltpu.VMEM(routes.shape, jnp.int32),
             pltpu.VMEM(gates.shape, f32),
@@ -577,7 +628,7 @@
             pltpu.VMEM((chunks, quarter, chunk), bf16),
             pltpu.VMEM((chunks, ring, block, chunk), bf16),
             pltpu.VMEM((chunks, ring, block, chunk), bf16),
-            dma((11,)),
+            dma((13,)),
             dma((ring,)),
             dma((ring,)),
             dma((ring,)),
@@ -611,6 +662,7 @@
         w_up,
         w_down,
     )
+    attn_out, moe_out = finished(attn_out, moe_out)
     return attn_out.reshape(query.shape), moe_out.reshape(hidden_in.shape)
 
 

time: 37.3 us -> 46 us (1.23)
  Pallas kernels: 33.3 us -> 45.1 us
  local copies, waits for them, and re-layouts: 3.14 us -> 0 us
    pallas_call x0 -> x1, Pallas kernels: none -> 11.1 us  [finished(): pl.pallas_call(finish_kernel, out_shape=(jax.ShapeDtypeStruct(attn_out.sh...]
    unnamed x2 -> x0, local copies, waits for them, and re-layouts: 3.14 us -> none
    pallas_call x1, Pallas kernels: 33.3 us -> 34.1 us  [dense_shards(): pl.pallas_call(functools.partial(layer_kernel, dims), out_shape=(jax.Shap...]
where the time goes in v3:
time: 46 us; the launch traced here: 45.8 us
  Pallas kernels  45.1 us (98%)
  between operations  0.64 us (1%)
    pallas_call x1, Pallas kernels, dense_shards(): pl.pallas_call(functools.partial(layer_kernel, dims), out_shape=(jax.Shap...  34.1 us
    pallas_call x1, Pallas kernels, finished(): pl.pallas_call(finish_kernel, out_shape=(jax.ShapeDtypeStruct(attn_out.sh...  11.1 us

profile of v3, /device:TPU:0, one launch (start us, length us, event | category | flops | bytes accessed | tf_op | source)
XLA Modules:
  0.0 45.8 jit_solution(5124371539027480983)
XLA Ops:
  0.6 34.1 %shard_map.131 = (bf16[16,8192]{1,0:T(8,128)(2,1)}, bf16[16,2048]{1,0:T(8,128)(2,1)}) custom-call(s32[2,8]{1,0:T(2,128)} %lengths_ref.1, bf16[16,2048]{1,0:T(8,128)(2,1)} %bitcast.7, s32[2,8,8]{2,1,0:T(8,128)} %routes_hbm.1, f32[2,8,8]{2,1,0:T(8,128)} %gates_hbm.1, bf16[16,8192]{1,0:T(8,128)(2,1)} %bitcast.6, bf16[16,512]{1,0:T(8,128)(2,1)} %bitcast.8, ...), custom_call_target="tpu_custom_call" | custom-call | flops 1207959552 | bytes 8388608 | tf_op jit(solution)/shard_map/pallas_call | solution.py:594
  34.7 11.1 %shard_map.132 = (bf16[16,8192]{1,0:T(8,128)(2,1)}, bf16[16,2048]{1,0:T(8,128)(2,1)}) custom-call(bf16[16,8192]{1,0:T(8,128)(2,1)} %get-tuple-element.6.attn_in, bf16[16,2048]{1,0:T(8,128)(2,1)} %get-tuple-element.7.moe_in), custom_call_target="tpu_custom_call" | custom-call | tf_op jit(solution)/shard_map/pallas_call | solution.py:545

commit v4 on v3

--- a/solution.py
+++ b/solution.py
@@ -214,6 +214,8 @@
     own_keys,
     own_values,
     row_weight,
+    gate_sum,
+    up_sum,
     act,
     keep_c,
     keep_x,
@@ -238,7 +240,7 @@
     rz_recv,
 ):
     batches, rows, width, heads, kv_heads, slots, experts, depth, chunks, chunk = dims
-    ring = gz_send.shape[0]
+    ring = gz_send.shape[1]
     block = batches * rows
     quarter = ring * block
     half = PAIR * quarter
@@ -316,40 +318,47 @@
         start = ((far_core * PAIR + far_side) * ring + step) * block
         return pl.ds(pl.multiple_of(start, block), block)
 
-    def gather_z(step):
+    cuts = (slice(0, width // 2), slice(width // 2, gathered.shape[1]))
+
+    def part_of(rows_at, part):
+        size = cuts[part].stop - cuts[part].start
+        return gathered.at[rows_at, pl.ds(cuts[part].start, size)]
+
+    def gather_z(part, step):
         return remote(
-            gathered.at[slot(0, 0, 0)],
-            gathered.at[slot(0, 0, step)],
-            gz_send.at[step],
-            gz_recv.at[step],
+            part_of(slot(0, 0, 0), part),
+            part_of(slot(0, 0, step), part),
+            gz_send.at[part, step],
+            gz_recv.at[part, step],
             up_by(step),
         )
 
-    def gather_x(step):
+    def gather_x(part, step):
         return remote(
-            gathered.at[slot(0, 0, step)],
-            gathered.at[slot(0, 1, step)],
-            gx_send.at[step],
-            gx_recv.at[step],
+            part_of(slot(0, 0, step), part),
+            part_of(slot(0, 1, step), part),
+            gx_send.at[part, step],
+            gx_recv.at[part, step],
             side,
         )
 
-    def gather_c(far_side, step):
+    def gather_c(part, far_side, step):
         return remote(
-            gathered.at[slot(0, far_side, step)],
-            gathered.at[slot(1, far_side, step)],
-            gc_send.at[far_side * ring + step],
-            gc_recv.at[far_side * ring + step],
+            part_of(slot(0, far_side, step), part),
+            part_of(slot(1, far_side, step), part),
+            gc_send.at[part, far_side * ring + step],
+            gc_recv.at[part, far_side * ring + step],
             mate,
         )
 
     order = list(range(1, ring))
     to_near = [nearest(turn) for turn in order]
     from_near = [lax.rem(ring - step, ring) for step in to_near]
-    for step in to_near:
-        gather_z(step).start()
-    gather_x(0).start()
-    gather_c(0, 0).start()
+    for part in range(2):
+        for step in to_near:
+            gather_z(part, step).start()
+        gather_x(part, 0).start()
+        gather_c(part, 0, 0).start()
 
     for load in loads[3:8]:
         load.wait()
@@ -402,37 +411,51 @@
         for _ in range(min(count, len(todo))):
             attend(todo.pop(0))
 
+    def forward_z(part, step):
+        gather_z(part, step).wait_recv()
+        gather_x(part, step).start()
+        gather_c(part, 0, step).start()
+
+    def forward_x(part, step):
+        gather_x(part, step).wait_recv()
+        gather_c(part, 1, step).start()
+
+    def arrived(part):
+        for far_side in range(PAIR):
+            for step in range(ring):
+                gather_c(part, far_side, step).wait_recv()
+
+    def units(part):
+        columns = slice(part * (width // 2), (part + 1) * (width // 2))
+        x = gathered[:, columns]
+        return (
+            jnp.dot(x, w_gate[0, columns, :], preferred_element_type=jnp.float32),
+            jnp.dot(x, w_up[0, columns, :], preferred_element_type=jnp.float32),
+        )
+
     for step in from_near:
-        gather_z(step).wait_recv()
-        gather_x(step).start()
-        gather_c(0, step).start()
+        forward_z(0, step)
         attend_some(2)
     for turn, step in enumerate([0] + from_near):
-        gather_x(step).wait_recv()
-        gather_c(1, step).start()
-        if turn % 2:
-            attend_some(2)
-
-    expert = me // PAIR
-
-    def hidden_units(far_core):
-        span = pl.ds(far_core * half, half)
-        x = gathered[span, 0:width]
-        gate_val = jnp.dot(x, w_gate[0], preferred_element_type=jnp.float32)
-        up_val = jnp.dot(x, w_up[0], preferred_element_type=jnp.float32)
-        act[span, :] = (gate_val / (1.0 + jnp.exp(-gate_val)) * up_val).astype(jnp.bfloat16)
-        tail = gathered[span, width:].astype(jnp.float32)
-        at = lax.broadcasted_iota(jnp.int32, tail.shape, 1)
-        mine = jnp.sum(jnp.where(lax.rem(at, experts) == expert, tail, 0.0), axis=1, keepdims=True)
-        row_weight[span, :] = jnp.broadcast_to(mine, (half, LANES))
-
+        forward_x(0, step)
+    for step in from_near:
+        forward_z(1, step)
+    attend_some(2)
     loads[8].wait()
     loads[9].wait()
-    hidden_units(0)
-    for far_side in range(PAIR):
-        for step in range(ring):
-            gather_c(far_side, step).wait_recv()
-    hidden_units(1)
+    arrived(0)
+    gate_sum[...], up_sum[...] = units(0)
+    for step in [0] + from_near:
+        forward_x(1, step)
+    arrived(1)
+    gate_val, up_val = units(1)
+    gate_val = gate_val + gate_sum[...]
+    up_val = up_val + up_sum[...]
+    act[...] = (gate_val / (1.0 + jnp.exp(-gate_val)) * up_val).astype(jnp.bfloat16)
+    tail = gathered[:, width:].astype(jnp.float32)
+    at = lax.broadcasted_iota(jnp.int32, tail.shape, 1)
+    mine = jnp.where(lax.rem(at, experts) == me // PAIR, tail, 0.0)
+    row_weight[...] = jnp.broadcast_to(jnp.sum(mine, axis=1, keepdims=True), row_weight.shape)
     loads[10].wait()
 
     def reduce_c(j):
@@ -510,12 +533,13 @@
     store_moe = pltpu.make_async_copy(moe_ref, moe_hbm, load_sems.at[12])
     store_moe.start()
 
-    for step in order:
-        gather_z(step).wait_send()
-    for step in range(ring):
-        gather_x(step).wait_send()
-        for far_side in range(PAIR):
-            gather_c(far_side, step).wait_send()
+    for part in range(2):
+        for step in order:
+            gather_z(part, step).wait_send()
+        for step in range(ring):
+            gather_x(part, step).wait_send()
+            for far_side in range(PAIR):
+                gather_c(part, far_side, step).wait_send()
     for j in range(chunks):
         reduce_c(j).wait_send()
         reduce_x(j).wait_send()
@@ -525,32 +549,21 @@
     store_moe.wait()
 
 
-def finish_kernel(attn_in, moe_in, attn_out, moe_out, sems):
-    copies = [pltpu.make_async_copy(moe_in, moe_out, sems.at[0])]
-    pieces = sems.shape[0] - 1
-    size = attn_in.shape[1] // pieces
-    for i in range(pieces):
-        span = pl.ds(i * size, size)
-        copies.append(
-            pltpu.make_async_copy(attn_in.at[:, span], attn_out.at[:, span], sems.at[1 + i])
-        )
-    for copy in copies:
-        copy.start()
-    for copy in copies:
-        copy.wait()
+def finish_kernel(attn_in, moe_in, attn_out, moe_out):
+    attn_out[...] = attn_in[...]
+    moe_out[...] = moe_in[...]
 
 
 def finished(attn_out, moe_out):
-    hbm = pl.BlockSpec(memory_space=pl.ANY)
+    vmem = pl.BlockSpec(memory_space=pltpu.VMEM)
     return pl.pallas_call(
         finish_kernel,
         out_shape=(
             jax.ShapeDtypeStruct(attn_out.shape, attn_out.dtype),
             jax.ShapeDtypeStruct(moe_out.shape, moe_out.dtype),
         ),
-        in_specs=[hbm, hbm],
-        out_specs=(hbm, hbm),
-        scratch_shapes=[pltpu.SemaphoreType.DMA((5,))],
+        in_specs=[vmem, vmem],
+        out_specs=(vmem, vmem),
         compiler_params=pltpu.CompilerParams(vmem_limit_bytes=63 * 1024 * 1024),
     )(attn_out, moe_out)
 
@@ -619,6 +632,8 @@
             pltpu.VMEM((block, fresh_key.shape[2]), f32),
             pltpu.VMEM((block, fresh_value.shape[2]), f32),
             pltpu.VMEM((PAIR * half, LANES), f32),
+            pltpu.VMEM((PAIR * half, depth), f32),
+            pltpu.VMEM((PAIR * half, depth), f32),
             pltpu.VMEM((PAIR * half, depth), bf16),
             pltpu.VMEM((chunks, half, chunk), f32),
             pltpu.VMEM((chunks, quarter, chunk), f32),
@@ -629,12 +644,12 @@
             pltpu.VMEM((chunks, ring, block, chunk), bf16),
             pltpu.VMEM((chunks, ring, block, chunk), bf16),
             dma((13,)),
-            dma((ring,)),
-            dma((ring,)),
-            dma((ring,)),
-            dma((ring,)),
-            dma((PAIR * ring,)),
-            dma((PAIR * ring,)),
+            dma((2, ring)),
+            dma((2, ring)),
+            dma((2, ring)),
+            dma((2, ring)),
+            dma((2, PAIR * ring)),
+            dma((2, PAIR * ring)),
             dma((chunks,)),
             dma((chunks,)),
             dma((chunks,)),

time: 46 us -> 38.3 us (0.83)
  Pallas kernels: 45.1 us -> 37.5 us
    pallas_call x1, Pallas kernels: 11.1 us -> 1.69 us  [finished(): pl.pallas_call(finish_kernel, out_shape=(jax.ShapeDtypeStruct(attn_out.sh...]
    pallas_call x1, Pallas kernels: 34.1 us -> 35.8 us  [dense_shards(): pl.pallas_call(functools.partial(layer_kernel, dims), out_shape=(jax.Shap...]
where the time goes in v4:
time: 38.3 us; the launch traced here: 38.1 us
  Pallas kernels  37.5 us (98%)
  between operations  0.64 us (2%)
    pallas_call x1, Pallas kernels, dense_shards(): pl.pallas_call(functools.partial(layer_kernel, dims), out_shape=(jax.Shap...  35.8 us
    pallas_call x1, Pallas kernels, finished(): pl.pallas_call(finish_kernel, out_shape=(jax.ShapeDtypeStruct(attn_out.sh...  1.69 us

profile of v4, /device:TPU:0, one launch (start us, length us, event | category | flops | bytes accessed | tf_op | source)
XLA Modules:
  0.0 38.1 jit_solution(17662634730421191940)
XLA Ops:
  0.6 35.8 %shard_map.131 = (bf16[16,8192]{1,0:T(8,128)(2,1)}, bf16[16,2048]{1,0:T(8,128)(2,1)}) custom-call(s32[2,8]{1,0:T(2,128)} %lengths_ref.1, bf16[16,2048]{1,0:T(8,128)(2,1)} %bitcast.7, s32[2,8,8]{2,1,0:T(8,128)} %routes_hbm.1, f32[2,8,8]{2,1,0:T(8,128)} %gates_hbm.1, bf16[16,8192]{1,0:T(8,128)(2,1)} %bitcast.6, bf16[16,512]{1,0:T(8,128)(2,1)} %bitcast.8, ...), custom_call_target="tpu_custom_call" | custom-call | flops 1207959552 | bytes 8388608 | tf_op jit(solution)/shard_map/pallas_call | solution.py:607
  36.5 1.7 %shard_map.132 = (bf16[16,8192]{1,0:T(8,128)(2,1)}, bf16[16,2048]{1,0:T(8,128)(2,1)}) custom-call(bf16[16,8192]{1,0:T(8,128)(2,1)} %get-tuple-element.6.attn_in, bf16[16,2048]{1,0:T(8,128)(2,1)} %get-tuple-element.7.moe_in), custom_call_target="tpu_custom_call" | custom-call | tf_op jit(solution)/shard_map/pallas_call | solution.py:559

commit v5 on v2

--- a/solution.py
+++ b/solution.py
@@ -193,6 +193,8 @@
     gate_hbm,
     up_hbm,
     down_hbm,
+    attn_hbm,
+    moe_hbm,
     attn_ref,
     moe_ref,
     hidden_ref,
@@ -303,7 +305,8 @@
     pl.semaphore_wait(barrier, len(others))
 
     def slot(far_core, far_side, step):
-        return pl.ds(((far_core * PAIR + far_side) * ring + step) * block, block)
+        start = ((far_core * PAIR + far_side) * ring + step) * block
+        return pl.ds(pl.multiple_of(start, block), block)
 
     def gather_z(step):
         return remote(
@@ -394,11 +397,10 @@
         gather_z(step).wait_recv()
         gather_x(step).start()
         gather_c(0, step).start()
-        attend_some(1)
+        attend_some(2)
     for step in [0] + order:
         gather_x(step).wait_recv()
         gather_c(1, step).start()
-        attend_some(1)
 
     expert = me // PAIR
 
@@ -480,17 +482,22 @@
             project(tick)
         if tick >= 2:
             after_c(tick - 2)
-    attend_some(2)
+    attend_some(4)
     for j in range(chunks):
         after_x(j)
-        attend_some(1)
+        if j == 0:
+            attend_some(4)
     attend_some(block)
     for h in range(heads):
         attn_ref[:, h * HEAD_SIZE : (h + 1) * HEAD_SIZE] = o_rows[
             h * block : (h + 1) * block, :
         ].astype(jnp.bfloat16)
+    store_attn = pltpu.make_async_copy(attn_ref, attn_hbm, load_sems.at[11])
+    store_attn.start()
     for j in range(chunks):
         after_z(j)
+    store_moe = pltpu.make_async_copy(moe_ref, moe_hbm, load_sems.at[12])
+    store_moe.start()
 
     for step in order:
         gather_z(step).wait_send()
@@ -503,6 +510,27 @@
         reduce_x(j).wait_send()
         for step in order:
             reduce_z(j, step).wait_send()
+    store_attn.wait()
+    store_moe.wait()
+
+
+def finish_kernel(attn_in, moe_in, attn_out, moe_out):
+    attn_out[...] = attn_in[...]
+    moe_out[...] = moe_in[...]
+
+
+def finished(attn_out, moe_out):
+    vmem = pl.BlockSpec(memory_space=pltpu.VMEM)
+    return pl.pallas_call(
+        finish_kernel,
+        out_shape=(
+            jax.ShapeDtypeStruct(attn_out.shape, attn_out.dtype),
+            jax.ShapeDtypeStruct(moe_out.shape, moe_out.dtype),
+        ),
+        in_specs=[vmem, vmem],
+        out_specs=(vmem, vmem),
+        compiler_params=pltpu.CompilerParams(vmem_limit_bytes=63 * 1024 * 1024),
+    )(attn_out, moe_out)
 
 
 def dense_shards(
@@ -527,16 +555,15 @@
     kv_heads = cached_key_rows.shape[3] // HEAD_SIZE
     heads = query.shape[2] // HEAD_SIZE
     depth = w_gate.shape[2]
-    chunks = 8
+    chunks = 4
     chunk = width // chunks
     block = batches * rows
     quarter = ring * block
     half = PAIR * quarter
     spread = -(-2 * experts // LANES) * LANES
     dims = (batches, rows, width, heads, kv_heads, slots, experts, depth, chunks, chunk)
-    vmem = pl.BlockSpec(memory_space=pltpu.VMEM)
     smem = pl.BlockSpec(memory_space=pltpu.SMEM)
-    anywhere = pl.BlockSpec(memory_space=pl.ANY)
+    hbm = pl.BlockSpec(memory_space=pl.ANY)
     bf16, f32 = jnp.bfloat16, jnp.float32
     dma = pltpu.SemaphoreType.DMA
     def flat(array):
@@ -548,9 +575,11 @@
             jax.ShapeDtypeStruct((block, query.shape[2]), bf16),
             jax.ShapeDtypeStruct((block, width), bf16),
         ),
-        in_specs=[smem] + [anywhere] * 11,
-        out_specs=(vmem, vmem),
+        in_specs=[smem] + [hbm] * 11,
+        out_specs=(hbm, hbm),
         scratch_shapes=[
+            pltpu.VMEM((block, query.shape[2]), bf16),
+            pltpu.VMEM((block, width), bf16),
             pltpu.VMEM((block, width), bf16),
             pltpu.VMEM(routes.shape, jnp.int32),
             pltpu.VMEM(gates.shape, f32),
@@ -577,7 +606,7 @@
             pltpu.VMEM((chunks, quarter, chunk), bf16),
             pltpu.VMEM((chunks, ring, block, chunk), bf16),
             pltpu.VMEM((chunks, ring, block, chunk), bf16),
-            dma((11,)),
+            dma((13,)),
             dma((ring,)),
             dma((ring,)),
             dma((ring,)),
@@ -611,6 +640,7 @@
         w_up,
         w_down,
     )
+    attn_out, moe_out = finished(attn_out, moe_out)
     return attn_out.reshape(query.shape), moe_out.reshape(hidden_in.shape)
 
 

time: 37.3 us -> 34.8 us (0.933)
  local copies, waits for them, and re-layouts: 3.14 us -> 0 us
  Pallas kernels: 33.3 us -> 34 us
    unnamed x2 -> x0, local copies, waits for them, and re-layouts: 3.14 us -> none
    pallas_call x0 -> x1, Pallas kernels: none -> 1.69 us  [finished(): pl.pallas_call(finish_kernel, out_shape=(jax.ShapeDtypeStruct(attn_out.sh...]
    pallas_call x1, Pallas kernels: 33.3 us -> 32.3 us  [dense_shards(): pl.pallas_call(functools.partial(layer_kernel, dims), out_shape=(jax.Shap...]
where the time goes in v5:
time: 34.8 us; the launch traced here: 34.6 us
  Pallas kernels  34 us (98%)
  between operations  0.64 us (2%)
    pallas_call x1, Pallas kernels, dense_shards(): pl.pallas_call(functools.partial(layer_kernel, dims), out_shape=(jax.Shap...  32.3 us
    pallas_call x1, Pallas kernels, finished(): pl.pallas_call(finish_kernel, out_shape=(jax.ShapeDtypeStruct(attn_out.sh...  1.69 us

profile of v5, /device:TPU:0, one launch (start us, length us, event | category | flops | bytes accessed | tf_op | source)
XLA Modules:
  0.0 34.6 jit_solution(6436975061318668269)
XLA Ops:
  0.6 32.3 %shard_map.131 = (bf16[16,8192]{1,0:T(8,128)(2,1)}, bf16[16,2048]{1,0:T(8,128)(2,1)}) custom-call(s32[2,8]{1,0:T(2,128)} %lengths_ref.1, bf16[16,2048]{1,0:T(8,128)(2,1)} %bitcast.7, s32[2,8,8]{2,1,0:T(8,128)} %routes_hbm.1, f32[2,8,8]{2,1,0:T(8,128)} %gates_hbm.1, bf16[16,8192]{1,0:T(8,128)(2,1)} %bitcast.6, bf16[16,512]{1,0:T(8,128)(2,1)} %bitcast.8, ...), custom_call_target="tpu_custom_call" | custom-call | flops 1207959552 | bytes 8388608 | tf_op jit(solution)/shard_map/pallas_call | solution.py:572
  33.0 1.7 %shard_map.132 = (bf16[16,8192]{1,0:T(8,128)(2,1)}, bf16[16,2048]{1,0:T(8,128)(2,1)}) custom-call(bf16[16,8192]{1,0:T(8,128)(2,1)} %get-tuple-element.6.attn_in, bf16[16,2048]{1,0:T(8,128)(2,1)} %get-tuple-element.7.moe_in), custom_call_target="tpu_custom_call" | custom-call | tf_op jit(solution)/shard_map/pallas_call | solution.py:524
